TPU v7x, 256 devices: a whole 4x4x8 slice. The times are simulated.
256 devices in a mesh: row: 32 (over y, z_lo, x), col: 8 (over z_hi, core).
Axes of the slice: x: 4, y: 4, z: 8 (z_hi: 4, z_lo: 2; z = z_hi * 2 + z_lo), core: 2. Of those that a mesh axis runs over, the one named last changes fastest.
Arguments:
- images: bfloat16 [20480, 1152], P(('row', 'col'))
- texts: bfloat16 [20480, 1152], P(('row', 'col'))
- image_ids: int32 [20480], replicated, may hold values from 0 to 10239, as said below
- text_ids: int32 [20480], replicated, may hold values from 0 to 10239, as said below
- temp_log: float32 [1], replicated, may hold values from 1.6 to 2.7
- bias: float32 [1], replicated, may hold values from -9 to -7
Outputs:
- image_grad: bfloat16 [20480, 1152], P(('row', 'col'))
- text_grad: bfloat16 [20480, 1152], P(('row', 'col'))
- scalars: float32 [3], replicated
Inputs may be any that keep to these rules, and one draw needn't show every extreme that they name: `image_ids`: every identity names exactly two image rows and exactly two text rows. `text_ids`: the text identities are a reordering of the image identities.
All inputs are finite; a program needn't handle non-finite values.
Results may differ from a plain program's by a relative error of at most 0.0035.
Values may be sent and summed in bfloat16 or wider, within the bound.
No kernel may reach another device: no remote copies, remote signals or barrier semaphores. Data moves between devices by JAX's collectives and lax.ppermute only.
A program may use at most 64 MiB of HBM per device.

v0:
```python
import functools
import itertools
import jax
import jax.numpy as jnp
from jax import lax
from jax.experimental import pallas as pl
from jax.experimental.pallas import tpu as pltpu
from jax.sharding import PartitionSpec as P

NX, NY, NZ, NC = 4, 4, 8, 2
LOG2E = 1.4426950408889634
F32, BF16 = jnp.float32, jnp.bfloat16
ANY = pl.BlockSpec(memory_space=pl.ANY)
VMEM = pl.BlockSpec(memory_space=pltpu.VMEM)
SMEM = pl.BlockSpec(memory_space=pltpu.SMEM)
BIG = pltpu.CompilerParams(vmem_limit_bytes=56 * 2**20)
SMALL = pltpu.CompilerParams(vmem_limit_bytes=24 * 2**20)
STAT_ROWS = 16


def linear(x, y, z, c):
    return (((y * 2 + z % 2) * NX + x) * (NZ // 2) + z // 2) * NC + c


def hop(a, move):
    pairs = []
    for x, y, z, c in itertools.product(range(NX), range(NY), range(NZ), range(NC)):
        dx, dy, dz, dc = move(c)
        to = linear((x + dx) % NX, (y + dy) % NY, (z + dz) % NZ, (c + dc) % NC)
        pairs.append((linear(x, y, z, c), to))
    return lax.ppermute(a, ("row", "col"), pairs)


def hop_first(a, k):
    return hop(a, lambda c: (0, k, 0, 0) if c else (k, 0, 0, 0))


def hop_second(a, k):
    return hop(a, lambda c: (k, 0, 0, 0) if c else (0, k, 0, 0))


def hop_z(a, k):
    return hop(a, lambda c: (0, 0, -k if c else k, 0))


def hop_core(a):
    return hop(a, lambda c: (0, 0, 0, 1))


def exchange(a, bit):
    return lax.ppermute(a, ("row", "col"), [(i, i ^ (1 << bit)) for i in range(256)])


def dot_t(a, b):
    return lax.dot_general(a, b, (((1,), (1,)), ((), ())), preferred_element_type=F32)


def dot_a(a, b):
    return lax.dot_general(a, b, (((0,), (0,)), ((), ())), preferred_element_type=F32)


def inverse_norm(rows):
    return lax.rsqrt(jnp.sum(rows * rows, axis=1, keepdims=True) + 1e-06)


def norm_kernel(x_ref, y_ref, xn_ref, yn_ref):
    for src, dst in ((x_ref, xn_ref), (y_ref, yn_ref)):
        rows = src[...].astype(F32)
        dst[...] = (rows * inverse_norm(rows)).astype(BF16)


def normalize(images, texts):
    like = jax.ShapeDtypeStruct(images.shape, BF16)
    return pl.pallas_call(
        norm_kernel,
        out_shape=(like, like),
        in_specs=[VMEM, VMEM],
        out_specs=(VMEM, VMEM),
        name="normalize",
        compiler_params=SMALL,
    )(images, texts)


def join_kernel(*refs):
    parts, out, sem = refs[:-2], refs[-2], refs[-1]
    at, copies = 0, []
    for i, part in enumerate(parts):
        rows = part.shape[0]
        copies.append(pltpu.make_async_copy(part, out.at[pl.ds(at, rows)], sem.at[i]))
        at += rows
    for copy in copies:
        copy.start()
    for copy in copies:
        copy.wait()


def join(parts):
    rows = sum(p.shape[0] for p in parts)
    return pl.pallas_call(
        join_kernel,
        out_shape=jax.ShapeDtypeStruct((rows, parts[0].shape[1]), parts[0].dtype),
        in_specs=[ANY] * len(parts),
        out_specs=ANY,
        scratch_shapes=[pltpu.SemaphoreType.DMA((len(parts),))],
        name="join",
        compiler_params=SMALL,
    )(*parts)


def load(refs, dst, sem, first):
    out, at = [], 0
    for ref in refs:
        rows = ref.shape[0]
        copy = pltpu.make_async_copy(ref, dst.at[pl.ds(at, rows)], sem.at[first + len(out)])
        copy.start()
        out.append((at, copy))
        at += rows
    return out


def fold(v):
    u = jnp.sum(v.reshape(v.shape[0] // 8, 8, v.shape[1]), axis=0)
    return sum(u[:, k : k + 128] for k in range(0, u.shape[1], 128))


def put_stats(sums, rows, width):
    row = lax.broadcasted_iota(jnp.int32, (STAT_ROWS, width), 0)
    v = jnp.where(row % 3 == 0, sums[0], jnp.where(row % 3 == 1, sums[1], sums[2]))
    high = v.astype(BF16).astype(F32)
    mid = (v - high).astype(BF16).astype(F32)
    low = v - high - mid
    v = jnp.where(row < 3, high, jnp.where(row < 6, mid, low))
    rows[...] = jnp.where(row < 9, v, 0.0).astype(BF16)


def get_stats(rows):
    v = rows[...].astype(F32)
    return (v[0:3] + v[3:6]) + v[6:9]


def tile_kernel(nx, nt, *refs):
    coef, image_ids, text_ids = refs[:3]
    images, texts = refs[3 : 3 + nx], refs[3 + nx : 3 + nx + nt]
    grad, gy, stats, xb, yb, prods, sem = refs[3 + nx + nt :]
    coming = load(texts, yb, sem, 0)
    coming_x = load(images, xb, sem, nt)
    for _, copy in coming:
        copy.wait()
    rows, cols = yb.shape[0], xb.shape[0]
    wide = 256
    steps = cols // wide
    scale, shift = coef[0] * LOG2E, coef[1] * LOG2E
    acc = [jnp.zeros((8, 128), F32)] * 3

    def multiply(k):
        while coming_x and coming_x[0][0] < (k + 1) * wide:
            coming_x.pop(0)[1].wait()
        prods[k % 2] = dot_t(yb[...], xb[k * wide : (k + 1) * wide])

    multiply(0)
    for k in range(steps):
        if k + 1 < steps:
            multiply(k + 1)
        dots = prods[k % 2]
        match = text_ids[:, :1] == image_ids[:1, k * wide : (k + 1) * wide]
        logits = dots * scale + shift
        e = jnp.exp2(jnp.where(match, -logits, logits))
        p = 1.0 + e
        s = e / p
        g = jnp.where(match, -s, s)
        grad[:, k * wide : (k + 1) * wide] = g.astype(BF16)
        acc[0] += fold(jnp.log2(p[: rows // 2] * p[rows // 2 :]))
        acc[1] += fold(g * dots)
        acc[2] += fold(g)
    for i in range(3):
        stats[i] = acc[i]
    part = rows // 2
    for r in range(0, rows, part):
        gy[r : r + part] = jnp.dot(
            grad[r : r + part], xb[...], preferred_element_type=F32
        ).astype(gy.dtype)


def tile(coef, image_ids, text_ids, images, texts, gy_dtype):
    cols, rows = image_ids.shape[1], text_ids.shape[0]
    d = images[0].shape[1]
    n = len(images) + len(texts)
    return pl.pallas_call(
        functools.partial(tile_kernel, len(images), len(texts)),
        out_shape=(
            jax.ShapeDtypeStruct((rows, cols), BF16),
            jax.ShapeDtypeStruct((rows, d), gy_dtype),
            jax.ShapeDtypeStruct((3, 8, 128), F32),
        ),
        in_specs=[SMEM, VMEM, VMEM] + [ANY] * n,
        out_specs=(VMEM, VMEM, VMEM),
        scratch_shapes=[
            pltpu.VMEM((cols, d), BF16),
            pltpu.VMEM((rows, d), BF16),
            pltpu.VMEM((2, rows, 256), F32),
            pltpu.SemaphoreType.DMA((n,)),
        ],
        name="tile",
        compiler_params=BIG,
    )(coef, image_ids, text_ids, *images, *texts)


def image_side_kernel(nt, ng, *refs):
    texts, grads = refs[:nt], refs[nt : nt + ng]
    stats_a, stats_b = refs[nt + ng : nt + ng + 2]
    outs, mine, (yb, gb, sem) = refs[nt + ng + 2 : -4], refs[-4], refs[-3:]
    coming = load(texts, yb, sem, 0) + load(grads, gb, sem, nt)
    sums = [jnp.sum(stats_a[i] + stats_b[i]) for i in range(3)]
    put_stats(sums, mine, mine.shape[1])
    for _, copy in coming:
        copy.wait()
    rows = outs[0].shape[0]
    for i, out in enumerate(outs):
        out[pl.ds(0, rows)] = dot_a(gb[:, i * rows : (i + 1) * rows], yb[...]).astype(out.dtype)
        if i:
            out[pl.ds(rows, STAT_ROWS)] = mine[...]


def image_side(texts, grads, stats):
    rows = sum(t.shape[0] for t in texts)
    d, cols = texts[0].shape[1], grads[0].shape[1]
    n = len(texts) + len(grads)
    size = cols // 4
    sent = jax.ShapeDtypeStruct((size + STAT_ROWS, d), BF16)
    return pl.pallas_call(
        functools.partial(image_side_kernel, len(texts), len(grads)),
        out_shape=(jax.ShapeDtypeStruct((size, d), F32), sent, sent, sent)
        + (jax.ShapeDtypeStruct((STAT_ROWS, d), BF16),),
        in_specs=[ANY] * n + [VMEM] * 2,
        out_specs=(VMEM,) * 5,
        scratch_shapes=[
            pltpu.VMEM((rows, d), BF16),
            pltpu.VMEM((rows, cols), BF16),
            pltpu.SemaphoreType.DMA((n,)),
        ],
        name="image_side",
        compiler_params=BIG,
    )(*texts, *grads, *stats)


def total_four(own, parts):
    return (own + parts[1]) + (parts[0] + parts[2])


def image_add_kernel(own, a, b, c, mine, keep, out1, out2, out3, sums):
    rows = keep.shape[0]
    for i, out in enumerate((keep, out1, out2, out3)):
        at = pl.ds(i * rows, rows)
        out[pl.ds(0, rows)] = (
            own[at] + a[at].astype(F32) + b[at].astype(F32) + c[at].astype(F32)
        ).astype(out.dtype)
    tail = pl.ds(4 * rows, STAT_ROWS)
    v = total_four(get_stats(mine), [get_stats(p.at[tail]) for p in (a, b, c)])
    put_stats([v[0:1], v[1:2], v[2:3]], sums, sums.shape[1])
    for out in (out1, out2, out3):
        out[pl.ds(rows, STAT_ROWS)] = sums[...]


def image_add(own, parts, mine):
    rows, d = own.shape[0] // 4, own.shape[1]
    sent = jax.ShapeDtypeStruct((rows + STAT_ROWS, d), BF16)
    return pl.pallas_call(
        image_add_kernel,
        out_shape=(jax.ShapeDtypeStruct((rows, d), F32), sent, sent, sent)
        + (jax.ShapeDtypeStruct((STAT_ROWS, d), BF16),),
        in_specs=[VMEM] * 5,
        out_specs=(VMEM,) * 5,
        name="image_add",
        compiler_params=SMALL,
    )(own, *parts, mine)


def text_add_kernel(own, other, keep, far, near, twice):
    at = 0
    for out in (keep, far, near, twice):
        rows = pl.ds(at, out.shape[0])
        out[...] = (own[rows] + other[rows].astype(F32)).astype(out.dtype)
        at += out.shape[0]


def text_add(own, other):
    rows, d = own.shape[0] // 8, own.shape[1]
    kinds = ((rows, F32), (rows, BF16), (2 * rows, F32), (4 * rows, BF16))
    return pl.pallas_call(
        text_add_kernel,
        out_shape=tuple(jax.ShapeDtypeStruct((r, d), t) for r, t in kinds),
        in_specs=[VMEM] * 2,
        out_specs=(VMEM,) * 4,
        name="text_add",
        compiler_params=SMALL,
    )(own, other)


def near_add_kernel(near, twice, out):
    rows = near.shape[0]
    out[...] = (near[...] + twice[pl.ds(rows, rows)].astype(F32)).astype(BF16)


def near_add(near, twice):
    return pl.pallas_call(
        near_add_kernel,
        out_shape=jax.ShapeDtypeStruct(near.shape, BF16),
        in_specs=[VMEM] * 2,
        out_specs=VMEM,
        name="near_add",
        compiler_params=SMALL,
    )(near, twice)


def other_add_kernel(near, twice, out):
    at = pl.ds(out.shape[0], out.shape[0])
    out[...] = near[at].astype(F32) + twice[at].astype(F32)


def other_add(near, twice):
    return pl.pallas_call(
        other_add_kernel,
        out_shape=jax.ShapeDtypeStruct((near.shape[0] // 2, near.shape[1]), F32),
        in_specs=[VMEM] * 2,
        out_specs=VMEM,
        name="other_add",
        compiler_params=SMALL,
    )(near, twice)


def finish_kernel(scale, *refs):
    raw, parts, out = refs[0], refs[1:-1], refs[-1]
    rows = raw[...].astype(F32)
    inv = inverse_norm(rows)
    unit = rows * inv
    owned = pl.ds(0, raw.shape[0])
    g = scale[0] * sum(p[owned].astype(F32) for p in parts)
    out[...] = (inv * (g - unit * jnp.sum(unit * g, axis=1, keepdims=True))).astype(BF16)


def finish(scale, raw, parts):
    return pl.pallas_call(
        finish_kernel,
        out_shape=jax.ShapeDtypeStruct(raw.shape, BF16),
        in_specs=[SMEM] + [VMEM] * (1 + len(parts)),
        out_specs=VMEM,
        name="finish",
        compiler_params=SMALL,
    )(scale, raw, *parts)


def stats_kernel(mine, a, b, c, out):
    tail = pl.ds(a.shape[0] - STAT_ROWS, STAT_ROWS)
    v = total_four(get_stats(mine), [get_stats(p.at[tail]) for p in (a, b, c)])
    out[...] = v[:, :128]


def stats_sum(mine, parts):
    return pl.pallas_call(
        stats_kernel,
        out_shape=jax.ShapeDtypeStruct((3, 128), F32),
        in_specs=[VMEM] * 4,
        out_specs=VMEM,
        name="stats_sum",
        compiler_params=SMALL,
    )(mine, *parts)


def labels(image_ids, text_ids, x, y, z, c, owned):
    split = (NY, 2, NX, NZ // 2, NC, owned)
    img = image_ids.reshape(split)[:, z % 2, :, z // 2, c].reshape(NY * NX, owned)
    txt = text_ids.reshape(split)[y, :, x].transpose(1, 0, 2, 3).reshape(NZ * NC, owned)
    first, second = jnp.where(c, y, x), jnp.where(c, x, y)
    at = []
    for j in range(4):
        for k in range(4):
            f, s = (first - k) % 4, (second - j) % 4
            at.append(jnp.where(c, f * NX + s, s * NX + f))
    img = img[jnp.stack(at)].reshape(1, -1)
    up = 1 - 2 * c
    at = []
    for core, sign in ((c, up), (1 - c, -up)):
        order = [(0, core), (4, core)] + [(k, d) for k in (1, 2, 3) for d in (core, 1 - core)]
        at += [(z - sign * k) % NZ * NC + d for k, d in order]
    txt = txt[jnp.stack(at)].reshape(-1, 1)
    return img, txt


def shards(images, texts, image_ids, text_ids, temp_log, bias):
    owned = images.shape[0]
    batch_all = owned * NX * NY * NZ * NC
    row, col = lax.axis_index("row"), lax.axis_index("col")
    x, y, z, c = row % NX, row // (2 * NX), 2 * (col // NC) + row // NX % 2, col % NC
    scale = jnp.exp(temp_log)
    coef = jnp.concatenate([scale, bias])
    img_ids, txt_ids = labels(image_ids, text_ids, x, y, z, c, owned)

    xn, yn = normalize(images, texts)
    sibling = hop_core(yn)
    near = [xn] + [hop_first(xn, k) for k in (1, 2, 3)]
    pair = join([yn, sibling])
    next_pair = hop_z(pair, 1)
    far = hop_z(yn, 4)
    near = join(near)
    twice = hop_z(join([pair, next_pair]), 2)
    image_blocks = [near] + [hop_second(near, k) for k in (1, 2, 3)]
    own = [yn, far, next_pair, twice]
    other = [sibling, hop_core(join(own[1:]))]

    half = NZ * owned
    g_own, gy_own, stats_own = tile(coef, img_ids, txt_ids[:half], image_blocks, own, F32)
    g_other, gy_other, stats_other = tile(coef, img_ids, txt_ids[half:], image_blocks, other, BF16)

    gy, far, near, twice = text_add(gy_own, hop_core(gy_other))
    twice, far = hop_z(twice, -2), hop_z(far, 4)
    near = hop_z(near_add(near, twice), -1)
    text_parts = [gy, twice, near, far, hop_core(other_add(near, twice))]

    keep, g1, g2, g3, stats = image_side(
        own + other, [g_own, g_other], [stats_own, stats_other]
    )
    parts = [hop_second(g, -k) for k, g in ((1, g1), (2, g2), (3, g3))]
    keep, g1, g2, g3, stats = image_add(keep, parts, stats)
    parts = [hop_first(g, -k) for k, g in ((1, g1), (2, g2), (3, g3))]

    stats = stats_sum(stats, parts)
    for bit in (5, 1, 2, 0):
        stats = stats + exchange(stats, bit)
    stats = stats[:, 0] * jnp.stack([jnp.float32(1 / LOG2E), scale[0], jnp.float32(1)])

    text_grad = finish(scale, texts, text_parts)
    image_grad = finish(scale, images, [keep] + parts)
    return image_grad, text_grad, stats / batch_all


def solution(mesh):
    spread = P(("row", "col"), None)
    return jax.shard_map(
        shards,
        mesh=mesh,
        in_specs=(spread, spread, P(), P(), P(), P()),
        out_specs=(spread, spread, P()),
        check_vma=False,
    )
```

profile of v0, /device:TPU:1, one launch (start us, length us, event | category | flops | bytes accessed | tf_op | source)
XLA Modules:
  0.0 190.1 jit_solution(8021148271709113878)
XLA Ops:
  0.6 0.9 copy-done.8
  1.6 0.9 copy-done.10
  2.7 3.3 %collective-permute-start.1 = (bf16[80,1152]{1,0:T(8,128)(2,1)S(1)}, bf16[80,1152]{1,0:T(8,128)(2,1)S(1)}, u32[]{:S(2)}, u32[]{:S(2)}) collective-permute-start(bf16[80,1152]{1,0:T(8,128)(2,1)S(1)} %get-tuple-element.25.refs_0_.refs_7_), channel_id=1, source_target_pairs={{0,1},{1,0},{32,33},{33,32},{2,3},{3,2},{34,35},{35,34},{4,5},{5,4... | collective-permute-start | bytes 552968 | tf_op jit(solution)/shard_map/ppermute | solution.py:31
  6.0 1.1 collective-permute-done.1.refs_1_.refs_7_.refs_4_
  7.0 0.5 join.4.refs_0_
  7.5 3.9 %collective-permute-start.2 = (bf16[160,1152]{1,0:T(8,128)(2,1)S(1)}, bf16[160,1152]{1,0:T(8,128)(2,1)S(1)}, u32[]{:S(2)}, u32[]{:S(2)}) collective-permute-start(bf16[160,1152]{1,0:T(8,128)(2,1)S(1)} %join.4.refs_0_), channel_id=1, source_target_pairs={{0,32},{1,39},{32,2},{33,1},{2,34},{3,33},{34,4},{35,3},{4,36},{5,... | collective-permute-start | bytes 1105928 | tf_op jit(solution)/shard_map/ppermute | solution.py:31
  11.4 4.5 %collective-permute-done.2.refs_1_.refs_9_.refs_2_ = bf16[160,1152]{1,0:T(8,128)(2,1)S(1)} collective-permute-done((bf16[160,1152]{1,0:T(8,128)(2,1)S(1)}, bf16[160,1152]{1,0:T(8,128)(2,1)S(1)}, u32[]{:S(2)}, u32[]{:S(2)}) %collective-permute-start.2) | collective-permute-done | bytes 368672 | tf_op jit(solution)/shard_map/ppermute | solution.py:31
  15.9 0.3 join.5
  16.2 2.7 %collective-permute-start.3 = (bf16[320,1152]{1,0:T(8,128)(2,1)S(1)}, bf16[320,1152]{1,0:T(8,128)(2,1)S(1)}, u32[]{:S(2)}, u32[]{:S(2)}) collective-permute-start(bf16[320,1152]{1,0:T(8,128)(2,1)S(1)} %join.5), channel_id=1, source_target_pairs={{0,2},{1,7},{32,34},{33,39},{2,4},{3,1},{34,36},{35,33},{4,6},{5,3... | collective-permute-start | bytes 2211848 | tf_op jit(solution)/shard_map/ppermute | solution.py:31
  19.0 1.0 collective-permute-start
  20.0 19.1 %collective-permute-done.refs_0_.refs_8_.refs_1_ = bf16[80,1152]{1,0:T(8,128)(2,1)S(1)} collective-permute-done((bf16[80,1152]{1,0:T(8,128)(2,1)S(1)}, bf16[80,1152]{1,0:T(8,128)(2,1)S(1)}, u32[]{:S(2)}, u32[]{:S(2)}) %collective-permute-start) | collective-permute-done | bytes 184352 | tf_op jit(solution)/shard_map/ppermute | solution.py:31
  39.1 0.7 join.6
  39.9 7.2 %collective-permute-start.4 = (bf16[560,1152]{1,0:T(8,128)(2,1)S(1)}, bf16[560,1152]{1,0:T(8,128)(2,1)}, u32[]{:S(2)}, u32[]{:S(2)}) collective-permute-start(bf16[560,1152]{1,0:T(8,128)(2,1)S(1)} %join.6), channel_id=1, source_target_pairs={{0,1},{1,0},{32,33},{33,32},{2,3},{3,2},{34,35},{35,34},{4,5},{5,4... | collective-permute-start | bytes 3870728 | tf_op jit(solution)/shard_map/ppermute | solution.py:31
  47.1 2.7 %collective-permute-start.7 = (bf16[80,1152]{1,0:T(8,128)(2,1)S(1)}, bf16[80,1152]{1,0:T(8,128)(2,1)S(1)}, u32[]{:S(2)}, u32[]{:S(2)}) collective-permute-start(bf16[80,1152]{1,0:T(8,128)(2,1)S(1)} %get-tuple-element.26.refs_0_), channel_id=1, source_target_pairs={{0,24},{1,193},{32,56},{33,225},{2,26},{3,195},{34,58},{35,227},{4... | collective-permute-start | bytes 552968 | tf_op jit(solution)/shard_map/ppermute | solution.py:31
  49.9 0.3 collective-permute-start.6
  50.2 0.7 collective-permute-start.5
  52.2 0.3 reshape.1255
  52.9 1.5 collective-permute-done.7.refs_3_
  54.3 1.8 collective-permute-done.6.refs_2_
  56.1 1.9 %collective-permute-done.5.refs_1_ = bf16[80,1152]{1,0:T(8,128)(2,1)S(1)} collective-permute-done((bf16[80,1152]{1,0:T(8,128)(2,1)S(1)}, bf16[80,1152]{1,0:T(8,128)(2,1)S(1)}, u32[]{:S(2)}, u32[]{:S(2)}) %collective-permute-start.5) | collective-permute-done | bytes 184352 | tf_op jit(solution)/shard_map/ppermute | solution.py:31
  58.0 1.0 join.7.refs_3_
  59.0 2.3 %collective-permute-start.10 = (bf16[320,1152]{1,0:T(8,128)(2,1)S(1)}, bf16[320,1152]{1,0:T(8,128)(2,1)S(1)}, u32[]{:S(2)}, u32[]{:S(2)}) collective-permute-start(bf16[320,1152]{1,0:T(8,128)(2,1)S(1)} %join.7.refs_3_), channel_id=1, source_target_pairs={{0,192},{1,25},{32,224},{33,57},{2,194},{3,27},{34,226},{35,59},{4... | collective-permute-start | bytes 2211848 | tf_op jit(solution)/shard_map/ppermute | solution.py:31
  61.3 0.5 collective-permute-start.9
  61.8 0.6 collective-permute-start.8
  62.4 0.6 gather_fusion
  63.0 0.7 reshape.1256.refs_1_
  63.6 0.3 reshape.1257
  64.0 0.6 gather_fusion.1
  64.6 0.9 slice.21.refs_2_
  65.4 0.6 pad_maximum_fusion.refs_0_
  66.0 11.5 %collective-permute-done.10.refs_6_ = bf16[320,1152]{1,0:T(8,128)(2,1)S(1)} collective-permute-done((bf16[320,1152]{1,0:T(8,128)(2,1)S(1)}, bf16[320,1152]{1,0:T(8,128)(2,1)S(1)}, u32[]{:S(2)}, u32[]{:S(2)}) %collective-permute-start.10) | collective-permute-done | bytes 737312 | tf_op jit(solution)/shard_map/ppermute | solution.py:31
  77.6 3.8 %collective-permute-done.8.refs_4_ = bf16[320,1152]{1,0:T(8,128)(2,1)} collective-permute-done((bf16[320,1152]{1,0:T(8,128)(2,1)S(1)}, bf16[320,1152]{1,0:T(8,128)(2,1)}, u32[]{:S(2)}, u32[]{:S(2)}) %collective-permute-start.8) | collective-permute-done | bytes 737312 | tf_op jit(solution)/shard_map/ppermute | solution.py:31
  81.4 11.3 %tile.3 = (bf16[640,1280]{1,0:T(8,128)(2,1)}, bf16[640,1152]{1,0:T(8,128)(2,1)}, f32[3,8,128]{2,1,0:T(8,128)}) custom-call(f32[2]{0:T(128)} %pad_maximum_fusion.refs_0_, s32[1,1280]{1,0:T(1,128)} %reshape.1256.refs_1_, s32[640,1]{1,0:T(8,128)} %slice.21.refs_2_, bf16[320,1152]{1,0:T(8,128)(2,1)} %copy-done.1, ...), custom_call_target="tpu_custom_call" | custom-call | tf_op jit(solution)/shard_map/tile/pallas_call | solution.py:188
  92.7 2.7 %collective-permute-start.17 = (bf16[640,1152]{1,0:T(8,128)(2,1)}, bf16[640,1152]{1,0:T(8,128)(2,1)S(1)}, u32[]{:S(2)}, u32[]{:S(2)}) collective-permute-start(bf16[640,1152]{1,0:T(8,128)(2,1)} %get-tuple-element.41), channel_id=1, source_target_pairs={{0,1},{1,0},{32,33},{33,32},{2,3},{3,2},{34,35},{35,34},{4,5},{5,4... | collective-permute-start | bytes 4423688 | tf_op jit(solution)/shard_map/ppermute | solution.py:31
  95.5 0.9 slice.20.refs_2_
  96.3 12.0 %tile.2 = (bf16[640,1280]{1,0:T(8,128)(2,1)}, f32[640,1152]{1,0:T(8,128)}, f32[3,8,128]{2,1,0:T(8,128)}) custom-call(f32[2]{0:T(128)} %pad_maximum_fusion.refs_0_, s32[1,1280]{1,0:T(1,128)} %reshape.1256.refs_1_, s32[640,1]{1,0:T(8,128)} %slice.20.refs_2_, bf16[320,1152]{1,0:T(8,128)(2,1)} %copy-done.1, bf16[320,1152]{1,0:T(8,128)(2,1)} %collective-permute-done.8.refs_4_, ...), custom_call_target="tpu_custom_call" | custom-call | tf_op jit(solution)/shard_map/tile/pallas_call | solution.py:188
  108.3 1.8 copy-done.3
  110.2 0.2 text_add.1
  110.4 3.4 %collective-permute-start.18 = (bf16[320,1152]{1,0:T(8,128)(2,1)S(1)}, bf16[320,1152]{1,0:T(8,128)(2,1)S(1)}, u32[]{:S(2)}, u32[]{:S(2)}) collective-permute-start(bf16[320,1152]{1,0:T(8,128)(2,1)S(1)} %get-tuple-element.43), channel_id=1, source_target_pairs={{0,6},{1,3},{32,38},{33,35},{2,0},{3,5},{34,32},{35,37},{4,2},{5,7... | collective-permute-start | bytes 2211848 | tf_op jit(solution)/shard_map/ppermute | solution.py:31
  113.8 9.5 %image_side.1 = (f32[320,1152]{1,0:T(8,128)}, bf16[336,1152]{1,0:T(8,128)(2,1)}, bf16[336,1152]{1,0:T(8,128)(2,1)}, bf16[336,1152]{1,0:T(8,128)(2,1)}, bf16[16,1152]{1,0:T(8,128)(2,1)}) custom-call(bf16[80,1152]{1,0:T(8,128)(2,1)} %copy-done.4, bf16[80,1152]{1,0:T(8,128)(2,1)} %copy-done.6, bf16[160,1152]{1,0:T(8,128)(2,1)} %copy-done.2, ...), custom_call_target="tpu_custom_call" | custom-call | tf_op jit(solution)/shard_map/image_side/pallas_call | solution.py:230
  123.4 0.4 collective-permute-start.11
  123.7 0.5 collective-permute-start.12
  124.3 0.7 collective-permute-start.13
  124.9 5.9 %collective-permute-done.18.twice.refs_2_ = bf16[320,1152]{1,0:T(8,128)(2,1)S(1)} collective-permute-done((bf16[320,1152]{1,0:T(8,128)(2,1)S(1)}, bf16[320,1152]{1,0:T(8,128)(2,1)S(1)}, u32[]{:S(2)}, u32[]{:S(2)}) %collective-permute-start.18) | collective-permute-done | bytes 737312 | tf_op jit(solution)/shard_map/ppermute | solution.py:31
  130.8 1.4 collective-permute-start.19
  132.2 2.4 %collective-permute-done.11.a = bf16[336,1152]{1,0:T(8,128)(2,1)S(1)} collective-permute-done((bf16[336,1152]{1,0:T(8,128)(2,1)}, bf16[336,1152]{1,0:T(8,128)(2,1)S(1)}, u32[]{:S(2)}, u32[]{:S(2)}) %collective-permute-start.11) | collective-permute-done | bytes 774176 | tf_op jit(solution)/shard_map/ppermute | solution.py:31
  134.7 1.8 collective-permute-done.12.b
  136.5 8.3 %collective-permute-done.13.c = bf16[336,1152]{1,0:T(8,128)(2,1)S(1)} collective-permute-done((bf16[336,1152]{1,0:T(8,128)(2,1)}, bf16[336,1152]{1,0:T(8,128)(2,1)S(1)}, u32[]{:S(2)}, u32[]{:S(2)}) %collective-permute-start.13) | collective-permute-done | bytes 774176 | tf_op jit(solution)/shard_map/ppermute | solution.py:31
  144.8 0.6 image_add.1
  145.4 0.4 collective-permute-start.14
  146.0 0.9 collective-permute-start.16
  146.9 3.4 %collective-permute-start.21 = (f32[80,1152]{1,0:T(8,128)S(1)}, f32[80,1152]{1,0:T(8,128)S(1)}, u32[]{:S(2)}, u32[]{:S(2)}) collective-permute-start(f32[80,1152]{1,0:T(8,128)S(1)} %other_add.1), channel_id=1, source_target_pairs={{0,1},{1,0},{32,33},{33,32},{2,3},{3,2},{34,35},{35,34},{4,5},{5,4... | collective-permute-start | bytes 1105928 | tf_op jit(solution)/shard_map/ppermute | solution.py:31
  150.3 1.8 collective-permute-done.15.refs_3_.b
  152.1 2.6 %collective-permute-done.16.refs_4_.c = bf16[96,1152]{1,0:T(8,128)(2,1)S(1)} collective-permute-done((bf16[96,1152]{1,0:T(8,128)(2,1)S(1)}, bf16[96,1152]{1,0:T(8,128)(2,1)S(1)}, u32[]{:S(2)}, u32[]{:S(2)}) %collective-permute-start.16) | collective-permute-done | bytes 221216 | tf_op jit(solution)/shard_map/ppermute | solution.py:31
  154.8 2.7 %collective-permute-done.22 = f32[3,128]{1,0:T(4,128)S(1)} collective-permute-done((f32[3,128]{1,0:T(4,128)S(1)}, f32[3,128]{1,0:T(4,128)S(1)}, u32[]{:S(2)}, u32[]{:S(2)}) %collective-permute-start.22) | collective-permute-done | bytes 1568 | tf_op jit(solution)/shard_map/ppermute | solution.py:51
  157.5 3.3 %collective-permute-done.23 = f32[3,128]{1,0:T(4,128)S(1)} collective-permute-done((f32[3,128]{1,0:T(4,128)S(1)}, f32[3,128]{1,0:T(4,128)S(1)}, u32[]{:S(2)}, u32[]{:S(2)}) %collective-permute-start.23) | collective-permute-done | bytes 1568 | tf_op jit(solution)/shard_map/ppermute | solution.py:51
  160.9 2.9 %collective-permute-start.24 = (f32[3,128]{1,0:T(4,128)S(1)}, f32[3,128]{1,0:T(4,128)S(1)}, u32[]{:S(2)}, u32[]{:S(2)}) collective-permute-start(f32[3,128]{1,0:T(4,128)S(1)} %add.377), channel_id=1, source_target_pairs={{0,4},{1,5},{2,6},{3,7},{4,0},{5,1},{6,2},{7,3},{8,12},{9,13},{10,... | collective-permute-start | bytes 4616 | tf_op jit(solution)/shard_map/ppermute | solution.py:51
  163.7 3.5 %collective-permute-done.24 = f32[3,128]{1,0:T(4,128)S(1)} collective-permute-done((f32[3,128]{1,0:T(4,128)S(1)}, f32[3,128]{1,0:T(4,128)S(1)}, u32[]{:S(2)}, u32[]{:S(2)}) %collective-permute-start.24) | collective-permute-done | bytes 1568 | tf_op jit(solution)/shard_map/ppermute | solution.py:51
  167.2 6.8 %collective-permute-start.25 = (f32[3,128]{1,0:T(4,128)S(1)}, f32[3,128]{1,0:T(4,128)S(1)}, u32[]{:S(2)}, u32[]{:S(2)}) collective-permute-start(f32[3,128]{1,0:T(4,128)S(1)} %add.378), channel_id=1, source_target_pairs={{0,1},{1,0},{2,3},{3,2},{4,5},{5,4},{6,7},{7,6},{8,9},{9,8},{10,11... | collective-permute-start | bytes 4616 | tf_op jit(solution)/shard_map/ppermute | solution.py:51
  174.0 0.9 finish.2
  175.1 2.3 %collective-permute-start.20 = (bf16[80,1152]{1,0:T(8,128)(2,1)S(1)}, bf16[80,1152]{1,0:T(8,128)(2,1)S(1)}, u32[]{:S(2)}, u32[]{:S(2)}) collective-permute-start(bf16[80,1152]{1,0:T(8,128)(2,1)S(1)} %get-tuple-element.45), channel_id=1, source_target_pairs={{0,4},{1,5},{32,36},{33,37},{2,6},{3,7},{34,38},{35,39},{4,0},{5,1... | collective-permute-start | bytes 552968 | tf_op jit(solution)/shard_map/ppermute | solution.py:31
  177.4 0.6 fusion.2
  178.0 11.2 %collective-permute-done.20.refs_4_ = bf16[80,1152]{1,0:T(8,128)(2,1)S(1)} collective-permute-done((bf16[80,1152]{1,0:T(8,128)(2,1)S(1)}, bf16[80,1152]{1,0:T(8,128)(2,1)S(1)}, u32[]{:S(2)}, u32[]{:S(2)}) %collective-permute-start.20) | collective-permute-done | bytes 184352 | tf_op jit(solution)/shard_map/ppermute | solution.py:31
  189.2 0.9 finish.3
  (58 shorter events, 1.1 us)
Async XLA Ops:
  0.6 0.9 copy-start.8
  1.6 0.9 copy-start.10
  2.6 37.2 %copy-start.4 = (bf16[80,1152]{1,0:T(8,128)(2,1)}, bf16[80,1152]{1,0:T(8,128)(2,1)S(1)}, u32[]{:S(2)}) copy-start(bf16[80,1152]{1,0:T(8,128)(2,1)S(1)} %get-tuple-element.25.refs_0_.refs_7_) | copy-start | bytes 552964
  2.7 4.4 %collective-permute-start.1 = (bf16[80,1152]{1,0:T(8,128)(2,1)S(1)}, bf16[80,1152]{1,0:T(8,128)(2,1)S(1)}, u32[]{:S(2)}, u32[]{:S(2)}) collective-permute-start(bf16[80,1152]{1,0:T(8,128)(2,1)S(1)} %get-tuple-element.25.refs_0_.refs_7_), channel_id=1, source_target_pairs={{0,1},{1,0},{32,33},{33,32},{2,3},{3,2},{34,35},{35,34},{4,5},{5,4... | collective-permute-start | bytes 552968 | tf_op jit(solution)/shard_map/ppermute | solution.py:31
  7.0 32.8 %copy-start.5 = (bf16[80,1152]{1,0:T(8,128)(2,1)}, bf16[80,1152]{1,0:T(8,128)(2,1)S(1)}, u32[]{:S(2)}) copy-start(bf16[80,1152]{1,0:T(8,128)(2,1)S(1)} %collective-permute-done.1.refs_1_.refs_7_.refs_4_) | copy-start | bytes 552964
  7.5 8.4 %collective-permute-start.2 = (bf16[160,1152]{1,0:T(8,128)(2,1)S(1)}, bf16[160,1152]{1,0:T(8,128)(2,1)S(1)}, u32[]{:S(2)}, u32[]{:S(2)}) collective-permute-start(bf16[160,1152]{1,0:T(8,128)(2,1)S(1)} %join.4.refs_0_), channel_id=1, source_target_pairs={{0,32},{1,39},{32,2},{33,1},{2,34},{3,33},{34,4},{35,3},{4,36},{5,... | collective-permute-start | bytes 1105928 | tf_op jit(solution)/shard_map/ppermute | solution.py:31
  15.9 24.0 %copy-start.2 = (bf16[160,1152]{1,0:T(8,128)(2,1)}, bf16[160,1152]{1,0:T(8,128)(2,1)S(1)}, u32[]{:S(2)}) copy-start(bf16[160,1152]{1,0:T(8,128)(2,1)S(1)} %collective-permute-done.2.refs_1_.refs_9_.refs_2_) | copy-start | bytes 1105924
  16.2 36.0 %copy-start.14 = (s32[20480]{0:T(1024)S(1)}, s32[20480]{0:T(1024)}, u32[]{:S(2)}) copy-start(s32[20480]{0:T(1024)} %param.8) | copy-start | bytes 245764
  16.2 22.9 %collective-permute-start.3 = (bf16[320,1152]{1,0:T(8,128)(2,1)S(1)}, bf16[320,1152]{1,0:T(8,128)(2,1)S(1)}, u32[]{:S(2)}, u32[]{:S(2)}) collective-permute-start(bf16[320,1152]{1,0:T(8,128)(2,1)S(1)} %join.5), channel_id=1, source_target_pairs={{0,2},{1,7},{32,34},{33,39},{2,4},{3,1},{34,36},{35,33},{4,6},{5,3... | collective-permute-start | bytes 2211848 | tf_op jit(solution)/shard_map/ppermute | solution.py:31
  19.0 20.1 %collective-permute-start = (bf16[80,1152]{1,0:T(8,128)(2,1)S(1)}, bf16[80,1152]{1,0:T(8,128)(2,1)S(1)}, u32[]{:S(2)}, u32[]{:S(2)}) collective-permute-start(bf16[80,1152]{1,0:T(8,128)(2,1)S(1)} %get-tuple-element.25.refs_0_.refs_7_), channel_id=1, source_target_pairs={{0,4},{1,5},{32,36},{33,37},{2,6},{3,7},{34,38},{35,39},{4,0},{5,1... | collective-permute-start | bytes 552968 | tf_op jit(solution)/shard_map/ppermute | solution.py:31
  39.1 11.8 %copy-start.6 = (bf16[80,1152]{1,0:T(8,128)(2,1)}, bf16[80,1152]{1,0:T(8,128)(2,1)S(1)}, u32[]{:S(2)}) copy-start(bf16[80,1152]{1,0:T(8,128)(2,1)S(1)} %collective-permute-done.refs_0_.refs_8_.refs_1_) | copy-start | bytes 552964
  39.1 11.8 %copy-start = (bf16[320,1152]{1,0:T(8,128)(2,1)}, bf16[320,1152]{1,0:T(8,128)(2,1)S(1)}, u32[]{:S(2)}) copy-start(bf16[320,1152]{1,0:T(8,128)(2,1)S(1)} %collective-permute-done.3.refs_2_.refs_10_.refs_3_) | copy-start | bytes 2211844
  39.9 23.8 %copy-start.15 = (s32[20480]{0:T(1024)S(1)}, s32[20480]{0:T(1024)}, u32[]{:S(2)}) copy-start(s32[20480]{0:T(1024)} %param.9) | copy-start | bytes 245764
  39.9 41.5 %collective-permute-start.4 = (bf16[560,1152]{1,0:T(8,128)(2,1)S(1)}, bf16[560,1152]{1,0:T(8,128)(2,1)}, u32[]{:S(2)}, u32[]{:S(2)}) collective-permute-start(bf16[560,1152]{1,0:T(8,128)(2,1)S(1)} %join.6), channel_id=1, source_target_pairs={{0,1},{1,0},{32,33},{33,32},{2,3},{3,2},{34,35},{35,34},{4,5},{5,4... | collective-permute-start | bytes 3870728 | tf_op jit(solution)/shard_map/ppermute | solution.py:31
  47.1 7.2 %collective-permute-start.7 = (bf16[80,1152]{1,0:T(8,128)(2,1)S(1)}, bf16[80,1152]{1,0:T(8,128)(2,1)S(1)}, u32[]{:S(2)}, u32[]{:S(2)}) collective-permute-start(bf16[80,1152]{1,0:T(8,128)(2,1)S(1)} %get-tuple-element.26.refs_0_), channel_id=1, source_target_pairs={{0,24},{1,193},{32,56},{33,225},{2,26},{3,195},{34,58},{35,227},{4... | collective-permute-start | bytes 552968 | tf_op jit(solution)/shard_map/ppermute | solution.py:31
  49.9 6.2 %collective-permute-start.6 = (bf16[80,1152]{1,0:T(8,128)(2,1)S(1)}, bf16[80,1152]{1,0:T(8,128)(2,1)S(1)}, u32[]{:S(2)}, u32[]{:S(2)}) collective-permute-start(bf16[80,1152]{1,0:T(8,128)(2,1)S(1)} %get-tuple-element.26.refs_0_), channel_id=1, source_target_pairs={{0,16},{1,129},{32,48},{33,161},{2,18},{3,131},{34,50},{35,163},{4... | collective-permute-start | bytes 552968 | tf_op jit(solution)/shard_map/ppermute | solution.py:31
  50.2 7.8 %collective-permute-start.5 = (bf16[80,1152]{1,0:T(8,128)(2,1)S(1)}, bf16[80,1152]{1,0:T(8,128)(2,1)S(1)}, u32[]{:S(2)}, u32[]{:S(2)}) collective-permute-start(bf16[80,1152]{1,0:T(8,128)(2,1)S(1)} %get-tuple-element.26.refs_0_), channel_id=1, source_target_pairs={{0,8},{1,65},{32,40},{33,97},{2,10},{3,67},{34,42},{35,99},{4,12},... | collective-permute-start | bytes 552968 | tf_op jit(solution)/shard_map/ppermute | solution.py:31
  59.0 22.4 %copy-start.1 = (bf16[320,1152]{1,0:T(8,128)(2,1)}, bf16[320,1152]{1,0:T(8,128)(2,1)S(1)}, u32[]{:S(2)}) copy-start(bf16[320,1152]{1,0:T(8,128)(2,1)S(1)} %join.7.refs_3_) | copy-start | bytes 2211844
  59.0 18.6 %collective-permute-start.10 = (bf16[320,1152]{1,0:T(8,128)(2,1)S(1)}, bf16[320,1152]{1,0:T(8,128)(2,1)S(1)}, u32[]{:S(2)}, u32[]{:S(2)}) collective-permute-start(bf16[320,1152]{1,0:T(8,128)(2,1)S(1)} %join.7.refs_3_), channel_id=1, source_target_pairs={{0,192},{1,25},{32,224},{33,57},{2,194},{3,27},{34,226},{35,59},{4... | collective-permute-start | bytes 2211848 | tf_op jit(solution)/shard_map/ppermute | solution.py:31
  61.3 16.3 %collective-permute-start.9 = (bf16[320,1152]{1,0:T(8,128)(2,1)S(1)}, bf16[320,1152]{1,0:T(8,128)(2,1)}, u32[]{:S(2)}, u32[]{:S(2)}) collective-permute-start(bf16[320,1152]{1,0:T(8,128)(2,1)S(1)} %join.7.refs_3_), channel_id=1, source_target_pairs={{0,128},{1,17},{32,160},{33,49},{2,130},{3,19},{34,162},{35,51},{4... | collective-permute-start | bytes 2211848 | tf_op jit(solution)/shard_map/ppermute | solution.py:31
  61.8 19.6 %collective-permute-start.8 = (bf16[320,1152]{1,0:T(8,128)(2,1)S(1)}, bf16[320,1152]{1,0:T(8,128)(2,1)}, u32[]{:S(2)}, u32[]{:S(2)}) collective-permute-start(bf16[320,1152]{1,0:T(8,128)(2,1)S(1)} %join.7.refs_3_), channel_id=1, source_target_pairs={{0,64},{1,9},{32,96},{33,41},{2,66},{3,11},{34,98},{35,43},{4,68},... | collective-permute-start | bytes 2211848 | tf_op jit(solution)/shard_map/ppermute | solution.py:31
  77.6 3.8 %copy-start.13 = (bf16[320,1152]{1,0:T(8,128)(2,1)}, bf16[320,1152]{1,0:T(8,128)(2,1)S(1)}, u32[]{:S(2)}) copy-start(bf16[320,1152]{1,0:T(8,128)(2,1)S(1)} %collective-permute-done.10.refs_6_) | copy-start | bytes 2211844
  92.7 15.6 %collective-permute-start.17 = (bf16[640,1152]{1,0:T(8,128)(2,1)}, bf16[640,1152]{1,0:T(8,128)(2,1)S(1)}, u32[]{:S(2)}, u32[]{:S(2)}) collective-permute-start(bf16[640,1152]{1,0:T(8,128)(2,1)} %get-tuple-element.41), channel_id=1, source_target_pairs={{0,1},{1,0},{32,33},{33,32},{2,3},{3,2},{34,35},{35,34},{4,5},{5,4... | collective-permute-start | bytes 4423688 | tf_op jit(solution)/shard_map/ppermute | solution.py:31
  108.3 1.8 copy-start.3
  110.4 20.4 %collective-permute-start.18 = (bf16[320,1152]{1,0:T(8,128)(2,1)S(1)}, bf16[320,1152]{1,0:T(8,128)(2,1)S(1)}, u32[]{:S(2)}, u32[]{:S(2)}) collective-permute-start(bf16[320,1152]{1,0:T(8,128)(2,1)S(1)} %get-tuple-element.43), channel_id=1, source_target_pairs={{0,6},{1,3},{32,38},{33,35},{2,0},{3,5},{34,32},{35,37},{4,2},{5,7... | collective-permute-start | bytes 2211848 | tf_op jit(solution)/shard_map/ppermute | solution.py:31
  123.3 21.4 %copy-start.7 = (f32[320,1152]{1,0:T(8,128)S(1)}, f32[320,1152]{1,0:T(8,128)}, u32[]{:S(2)}) copy-start(f32[320,1152]{1,0:T(8,128)} %get-tuple-element.31.own) | copy-start | bytes 4423684
  123.4 21.4 %copy-start.12 = (bf16[16,1152]{1,0:T(8,128)(2,1)S(1)}, bf16[16,1152]{1,0:T(8,128)(2,1)}, u32[]{:S(2)}) copy-start(bf16[16,1152]{1,0:T(8,128)(2,1)} %get-tuple-element.35.mine) | copy-start | bytes 110596
  123.4 11.3 %collective-permute-start.11 = (bf16[336,1152]{1,0:T(8,128)(2,1)}, bf16[336,1152]{1,0:T(8,128)(2,1)S(1)}, u32[]{:S(2)}, u32[]{:S(2)}) collective-permute-start(bf16[336,1152]{1,0:T(8,128)(2,1)} %get-tuple-element.32), channel_id=1, source_target_pairs={{0,192},{1,25},{32,224},{33,57},{2,194},{3,27},{34,226},{35,59},{4... | collective-permute-start | bytes 2322440 | tf_op jit(solution)/shard_map/ppermute | solution.py:31
  123.7 12.8 %collective-permute-start.12 = (bf16[336,1152]{1,0:T(8,128)(2,1)}, bf16[336,1152]{1,0:T(8,128)(2,1)S(1)}, u32[]{:S(2)}, u32[]{:S(2)}) collective-permute-start(bf16[336,1152]{1,0:T(8,128)(2,1)} %get-tuple-element.33), channel_id=1, source_target_pairs={{0,128},{1,17},{32,160},{33,49},{2,130},{3,19},{34,162},{35,51},{4... | collective-permute-start | bytes 2322440 | tf_op jit(solution)/shard_map/ppermute | solution.py:31
  124.3 20.5 %collective-permute-start.13 = (bf16[336,1152]{1,0:T(8,128)(2,1)}, bf16[336,1152]{1,0:T(8,128)(2,1)S(1)}, u32[]{:S(2)}, u32[]{:S(2)}) collective-permute-start(bf16[336,1152]{1,0:T(8,128)(2,1)} %get-tuple-element.34), channel_id=1, source_target_pairs={{0,64},{1,9},{32,96},{33,41},{2,66},{3,11},{34,98},{35,43},{4,68},... | collective-permute-start | bytes 2322440 | tf_op jit(solution)/shard_map/ppermute | solution.py:31
  130.8 16.1 %collective-permute-start.19 = (bf16[160,1152]{1,0:T(8,128)(2,1)S(1)}, bf16[160,1152]{1,0:T(8,128)(2,1)S(1)}, u32[]{:S(2)}, u32[]{:S(2)}) collective-permute-start(bf16[160,1152]{1,0:T(8,128)(2,1)S(1)} %near_add.1), channel_id=1, source_target_pairs={{0,38},{1,33},{32,0},{33,3},{2,32},{3,35},{34,2},{35,5},{4,34},{5,... | collective-permute-start | bytes 1105928 | tf_op jit(solution)/shard_map/ppermute | solution.py:31
  145.3 28.7 %copy-start.9 = (bf16[80,1152]{1,0:T(8,128)(2,1)S(1)}, bf16[80,1152]{1,0:T(8,128)(2,1)}, u32[]{:S(2)}) copy-start(bf16[80,1152]{1,0:T(8,128)(2,1)} %refs_0_.2) | copy-start | bytes 552964
  145.4 5.0 %collective-permute-start.14 = (bf16[96,1152]{1,0:T(8,128)(2,1)S(1)}, bf16[96,1152]{1,0:T(8,128)(2,1)S(1)}, u32[]{:S(2)}, u32[]{:S(2)}) collective-permute-start(bf16[96,1152]{1,0:T(8,128)(2,1)S(1)} %get-tuple-element.37), channel_id=1, source_target_pairs={{0,24},{1,193},{32,56},{33,225},{2,26},{3,195},{34,58},{35,227},{4... | collective-permute-start | bytes 663560 | tf_op jit(solution)/shard_map/ppermute | solution.py:31
  145.7 6.4 %collective-permute-start.15 = (bf16[96,1152]{1,0:T(8,128)(2,1)S(1)}, bf16[96,1152]{1,0:T(8,128)(2,1)S(1)}, u32[]{:S(2)}, u32[]{:S(2)}) collective-permute-start(bf16[96,1152]{1,0:T(8,128)(2,1)S(1)} %get-tuple-element.38), channel_id=1, source_target_pairs={{0,16},{1,129},{32,48},{33,161},{2,18},{3,131},{34,50},{35,163},{4... | collective-permute-start | bytes 663560 | tf_op jit(solution)/shard_map/ppermute | solution.py:31
  145.9 43.2 %copy-start.11 = (bf16[80,1152]{1,0:T(8,128)(2,1)S(1)}, bf16[80,1152]{1,0:T(8,128)(2,1)}, u32[]{:S(2)}) copy-start(bf16[80,1152]{1,0:T(8,128)(2,1)} %refs_0_.3) | copy-start | bytes 552964
  146.0 8.7 %collective-permute-start.16 = (bf16[96,1152]{1,0:T(8,128)(2,1)S(1)}, bf16[96,1152]{1,0:T(8,128)(2,1)S(1)}, u32[]{:S(2)}, u32[]{:S(2)}) collective-permute-start(bf16[96,1152]{1,0:T(8,128)(2,1)S(1)} %get-tuple-element.39), channel_id=1, source_target_pairs={{0,8},{1,65},{32,40},{33,97},{2,10},{3,67},{34,42},{35,99},{4,12},... | collective-permute-start | bytes 663560 | tf_op jit(solution)/shard_map/ppermute | solution.py:31
  146.9 42.2 %collective-permute-start.21 = (f32[80,1152]{1,0:T(8,128)S(1)}, f32[80,1152]{1,0:T(8,128)S(1)}, u32[]{:S(2)}, u32[]{:S(2)}) collective-permute-start(f32[80,1152]{1,0:T(8,128)S(1)} %other_add.1), channel_id=1, source_target_pairs={{0,1},{1,0},{32,33},{33,32},{2,3},{3,2},{34,35},{35,34},{4,5},{5,4... | collective-permute-start | bytes 1105928 | tf_op jit(solution)/shard_map/ppermute | solution.py:31
  154.7 2.8 %collective-permute-start.22 = (f32[3,128]{1,0:T(4,128)S(1)}, f32[3,128]{1,0:T(4,128)S(1)}, u32[]{:S(2)}, u32[]{:S(2)}) collective-permute-start(f32[3,128]{1,0:T(4,128)S(1)} %stats_sum.1), channel_id=1, source_target_pairs={{0,32},{1,33},{2,34},{3,35},{4,36},{5,37},{6,38},{7,39},{8,40},{9,... | collective-permute-start | bytes 4616 | tf_op jit(solution)/shard_map/ppermute | solution.py:51
  157.5 3.3 %collective-permute-start.23 = (f32[3,128]{1,0:T(4,128)S(1)}, f32[3,128]{1,0:T(4,128)S(1)}, u32[]{:S(2)}, u32[]{:S(2)}) collective-permute-start(f32[3,128]{1,0:T(4,128)S(1)} %add.376), channel_id=1, source_target_pairs={{0,2},{1,3},{2,0},{3,1},{4,6},{5,7},{6,4},{7,5},{8,10},{9,11},{10,... | collective-permute-start | bytes 4616 | tf_op jit(solution)/shard_map/ppermute | solution.py:51
  160.9 6.3 %collective-permute-start.24 = (f32[3,128]{1,0:T(4,128)S(1)}, f32[3,128]{1,0:T(4,128)S(1)}, u32[]{:S(2)}, u32[]{:S(2)}) collective-permute-start(f32[3,128]{1,0:T(4,128)S(1)} %add.377), channel_id=1, source_target_pairs={{0,4},{1,5},{2,6},{3,7},{4,0},{5,1},{6,2},{7,3},{8,12},{9,13},{10,... | collective-permute-start | bytes 4616 | tf_op jit(solution)/shard_map/ppermute | solution.py:51
  167.2 7.7 %collective-permute-start.25 = (f32[3,128]{1,0:T(4,128)S(1)}, f32[3,128]{1,0:T(4,128)S(1)}, u32[]{:S(2)}, u32[]{:S(2)}) collective-permute-start(f32[3,128]{1,0:T(4,128)S(1)} %add.378), channel_id=1, source_target_pairs={{0,1},{1,0},{2,3},{3,2},{4,5},{5,4},{6,7},{7,6},{8,9},{9,8},{10,11... | collective-permute-start | bytes 4616 | tf_op jit(solution)/shard_map/ppermute | solution.py:51
  175.1 14.1 %collective-permute-start.20 = (bf16[80,1152]{1,0:T(8,128)(2,1)S(1)}, bf16[80,1152]{1,0:T(8,128)(2,1)S(1)}, u32[]{:S(2)}, u32[]{:S(2)}) collective-permute-start(bf16[80,1152]{1,0:T(8,128)(2,1)S(1)} %get-tuple-element.45), channel_id=1, source_target_pairs={{0,4},{1,5},{32,36},{33,37},{2,6},{3,7},{34,38},{35,39},{4,0},{5,1... | collective-permute-start | bytes 552968 | tf_op jit(solution)/shard_map/ppermute | solution.py:31
where the time goes:
time: 190 us
  waiting for transfers between devices  88.7 us (47%)
  starting transfers between devices  51.4 us (27%)
  Pallas kernels  38.2 us (20%)
  local copies, waits for them, and re-layouts  8.22 us (4%)
  between operations  2.35 us (1%)
    ppermute x22, waiting for transfers between devices, hop(): return lax.ppermute(a, ('row', 'col'), pairs)  79.1 us
    ppermute x22, starting transfers between devices, hop(): return lax.ppermute(a, ('row', 'col'), pairs)  41.7 us
    pallas_call x2, Pallas kernels, tile(): pl.pallas_call(functools.partial(tile_kernel, len(images), len(texts)), o...  23.3 us
    ppermute x4, starting transfers between devices, exchange(): lax.ppermute(a, ('row', 'col'), [(i, i ^ 1 << bit) for i in range(256)])  9.73 us
    ppermute x4, waiting for transfers between devices, exchange(): lax.ppermute(a, ('row', 'col'), [(i, i ^ 1 << bit) for i in range(256)])  9.54 us
    pallas_call x1, Pallas kernels, image_side(): pl.pallas_call(functools.partial(image_side_kernel, len(texts), len(grads...  9.49 us
  transfers between devices with their start and end apart: 26, of which 18 were waited for; matrix products, arithmetic and copies ran while one was open for 3% of the time, Pallas kernels for 13%

commit v1 on v0

--- a/solution.py
+++ b/solution.py
@@ -47,8 +47,9 @@
     return hop(a, lambda c: (0, 0, 0, 1))
 
 
-def exchange(a, bit):
-    return lax.ppermute(a, ("row", "col"), [(i, i ^ (1 << bit)) for i in range(256)])
+def exchange(a, bit0, bit1):
+    pairs = [(i, i ^ (1 << (bit1 if i % 2 else bit0))) for i in range(256)]
+    return lax.ppermute(a, ("row", "col"), pairs)
 
 
 def dot_t(a, b):
@@ -81,8 +82,8 @@
     )(images, texts)
 
 
-def join_kernel(*refs):
-    parts, out, sem = refs[:-2], refs[-2], refs[-1]
+def join_kernel(n, *refs):
+    parts, out, sem = refs[:n], refs[-2], refs[-1]
     at, copies = 0, []
     for i, part in enumerate(parts):
         rows = part.shape[0]
@@ -94,17 +95,17 @@
         copy.wait()
 
 
-def join(parts):
+def join(parts, after=()):
     rows = sum(p.shape[0] for p in parts)
     return pl.pallas_call(
-        join_kernel,
+        functools.partial(join_kernel, len(parts)),
         out_shape=jax.ShapeDtypeStruct((rows, parts[0].shape[1]), parts[0].dtype),
-        in_specs=[ANY] * len(parts),
+        in_specs=[ANY] * (len(parts) + len(after)),
         out_specs=ANY,
         scratch_shapes=[pltpu.SemaphoreType.DMA((len(parts),))],
         name="join",
         compiler_params=SMALL,
-    )(*parts)
+    )(*parts, *after)
 
 
 def load(refs, dst, sem, first):
@@ -138,10 +139,10 @@
     return (v[0:3] + v[3:6]) + v[6:9]
 
 
-def tile_kernel(nx, nt, *refs):
-    coef, image_ids, text_ids = refs[:3]
-    images, texts = refs[3 : 3 + nx], refs[3 + nx : 3 + nx + nt]
-    grad, gy, stats, xb, yb, prods, sem = refs[3 + nx + nt :]
+def tile_kernel(nx, nt, last, *refs):
+    coef, image_ids, text_ids, before = refs[:4]
+    images, texts = refs[4 : 4 + nx], refs[4 + nx : 4 + nx + nt]
+    grad, keep, send, stats, xb, yb, prods, sem = refs[4 + nx + nt :]
     coming = load(texts, yb, sem, 0)
     coming_x = load(images, xb, sem, nt)
     for _, copy in coming:
@@ -150,7 +151,7 @@
     wide = 256
     steps = cols // wide
     scale, shift = coef[0] * LOG2E, coef[1] * LOG2E
-    acc = [jnp.zeros((8, 128), F32)] * 3
+    acc = [before[i] for i in range(3)]
 
     def multiply(k):
         while coming_x and coming_x[0][0] < (k + 1) * wide:
@@ -173,143 +174,144 @@
         acc[1] += fold(g * dots)
         acc[2] += fold(g)
     for i in range(3):
-        stats[i] = acc[i]
+        if last:
+            stats[pl.ds(i, 1)] = jnp.full((1, 128), jnp.sum(acc[i]))
+        else:
+            stats[i] = acc[i]
     part = rows // 2
-    for r in range(0, rows, part):
-        gy[r : r + part] = jnp.dot(
+    for r, out in ((part, send), (0, keep)):
+        out[...] = jnp.dot(
             grad[r : r + part], xb[...], preferred_element_type=F32
-        ).astype(gy.dtype)
-
-
-def tile(coef, image_ids, text_ids, images, texts, gy_dtype):
+        ).astype(out.dtype)
+
+
+def tile(coef, image_ids, text_ids, before, images, texts, last):
     cols, rows = image_ids.shape[1], text_ids.shape[0]
     d = images[0].shape[1]
     n = len(images) + len(texts)
     return pl.pallas_call(
-        functools.partial(tile_kernel, len(images), len(texts)),
+        functools.partial(tile_kernel, len(images), len(texts), last),
         out_shape=(
             jax.ShapeDtypeStruct((rows, cols), BF16),
-            jax.ShapeDtypeStruct((rows, d), gy_dtype),
-            jax.ShapeDtypeStruct((3, 8, 128), F32),
+            jax.ShapeDtypeStruct((rows // 2, d), F32),
+            jax.ShapeDtypeStruct((rows // 2, d), BF16),
+            jax.ShapeDtypeStruct((3, 128) if last else (3, 8, 128), F32),
         ),
-        in_specs=[SMEM, VMEM, VMEM] + [ANY] * n,
-        out_specs=(VMEM, VMEM, VMEM),
+        in_specs=[SMEM, VMEM, VMEM, VMEM] + [ANY] * n,
+        out_specs=(VMEM,) * 4,
         scratch_shapes=[
             pltpu.VMEM((cols, d), BF16),
             pltpu.VMEM((rows, d), BF16),
             pltpu.VMEM((2, rows, 256), F32),
             pltpu.SemaphoreType.DMA((n,)),
         ],
-        name="tile",
+        name="tile_late" if last else "tile_early",
+        cost_estimate=pl.CostEstimate(
+            flops=4 * rows * cols * d, bytes_accessed=8 * cols * d, transcendentals=3 * rows * cols
+        ),
         compiler_params=BIG,
-    )(coef, image_ids, text_ids, *images, *texts)
+    )(coef, image_ids, text_ids, before, *images, *texts)
 
 
 def image_side_kernel(nt, ng, *refs):
     texts, grads = refs[:nt], refs[nt : nt + ng]
-    stats_a, stats_b = refs[nt + ng : nt + ng + 2]
-    outs, mine, (yb, gb, sem) = refs[nt + ng + 2 : -4], refs[-4], refs[-3:]
-    coming = load(texts, yb, sem, 0) + load(grads, gb, sem, nt)
-    sums = [jnp.sum(stats_a[i] + stats_b[i]) for i in range(3)]
-    put_stats(sums, mine, mine.shape[1])
-    for _, copy in coming:
+    outs, (yb, gb, sem) = refs[-7:-3], refs[-3:]
+    for _, copy in load(texts, yb, sem, 0) + load(grads, gb, sem, nt):
         copy.wait()
     rows = outs[0].shape[0]
-    for i, out in enumerate(outs):
-        out[pl.ds(0, rows)] = dot_a(gb[:, i * rows : (i + 1) * rows], yb[...]).astype(out.dtype)
-        if i:
-            out[pl.ds(rows, STAT_ROWS)] = mine[...]
-
-
-def image_side(texts, grads, stats):
+    for i in (1, 2, 3, 0):
+        at = slice(i * rows, (i + 1) * rows)
+        outs[i][...] = dot_a(gb[:, at], yb[...]).astype(outs[i].dtype)
+
+
+def image_side(texts, grads, after):
     rows = sum(t.shape[0] for t in texts)
     d, cols = texts[0].shape[1], grads[0].shape[1]
     n = len(texts) + len(grads)
     size = cols // 4
-    sent = jax.ShapeDtypeStruct((size + STAT_ROWS, d), BF16)
+    sent = jax.ShapeDtypeStruct((size, d), BF16)
     return pl.pallas_call(
         functools.partial(image_side_kernel, len(texts), len(grads)),
-        out_shape=(jax.ShapeDtypeStruct((size, d), F32), sent, sent, sent)
-        + (jax.ShapeDtypeStruct((STAT_ROWS, d), BF16),),
-        in_specs=[ANY] * n + [VMEM] * 2,
-        out_specs=(VMEM,) * 5,
+        out_shape=(jax.ShapeDtypeStruct((size, d), F32), sent, sent, sent),
+        in_specs=[ANY] * (n + len(after)),
+        out_specs=(VMEM,) * 4,
         scratch_shapes=[
             pltpu.VMEM((rows, d), BF16),
             pltpu.VMEM((rows, cols), BF16),
             pltpu.SemaphoreType.DMA((n,)),
         ],
         name="image_side",
+        cost_estimate=pl.CostEstimate(
+            flops=2 * rows * cols * d, bytes_accessed=8 * cols * d, transcendentals=0
+        ),
         compiler_params=BIG,
-    )(*texts, *grads, *stats)
+    )(*texts, *grads, *after)
 
 
 def total_four(own, parts):
     return (own + parts[1]) + (parts[0] + parts[2])
 
 
-def image_add_kernel(own, a, b, c, mine, keep, out1, out2, out3, sums):
+def image_add_kernel(own, a, b, c, stats, keep, out1, out2, out3):
     rows = keep.shape[0]
+    sums = [stats[pl.ds(i, 1)][:, :1] for i in range(3)]
     for i, out in enumerate((keep, out1, out2, out3)):
         at = pl.ds(i * rows, rows)
         out[pl.ds(0, rows)] = (
             own[at] + a[at].astype(F32) + b[at].astype(F32) + c[at].astype(F32)
         ).astype(out.dtype)
-    tail = pl.ds(4 * rows, STAT_ROWS)
-    v = total_four(get_stats(mine), [get_stats(p.at[tail]) for p in (a, b, c)])
-    put_stats([v[0:1], v[1:2], v[2:3]], sums, sums.shape[1])
-    for out in (out1, out2, out3):
-        out[pl.ds(rows, STAT_ROWS)] = sums[...]
-
-
-def image_add(own, parts, mine):
+        if i:
+            put_stats(sums, out.at[pl.ds(rows, STAT_ROWS)], out.shape[1])
+
+
+def image_add(own, parts, stats):
     rows, d = own.shape[0] // 4, own.shape[1]
     sent = jax.ShapeDtypeStruct((rows + STAT_ROWS, d), BF16)
     return pl.pallas_call(
         image_add_kernel,
-        out_shape=(jax.ShapeDtypeStruct((rows, d), F32), sent, sent, sent)
-        + (jax.ShapeDtypeStruct((STAT_ROWS, d), BF16),),
+        out_shape=(jax.ShapeDtypeStruct((rows, d), F32), sent, sent, sent),
         in_specs=[VMEM] * 5,
-        out_specs=(VMEM,) * 5,
+        out_specs=(VMEM,) * 4,
         name="image_add",
         compiler_params=SMALL,
-    )(own, *parts, mine)
-
-
-def text_add_kernel(own, other, keep, far, near, twice):
+    )(own, *parts, stats)
+
+
+def text_add_kernel(own, other, *outs):
     at = 0
-    for out in (keep, far, near, twice):
+    for out in outs:
         rows = pl.ds(at, out.shape[0])
         out[...] = (own[rows] + other[rows].astype(F32)).astype(out.dtype)
         at += out.shape[0]
 
 
-def text_add(own, other):
-    rows, d = own.shape[0] // 8, own.shape[1]
-    kinds = ((rows, F32), (rows, BF16), (2 * rows, F32), (4 * rows, BF16))
+def text_add(own, other, kinds):
+    d = own.shape[1]
     return pl.pallas_call(
         text_add_kernel,
         out_shape=tuple(jax.ShapeDtypeStruct((r, d), t) for r, t in kinds),
         in_specs=[VMEM] * 2,
-        out_specs=(VMEM,) * 4,
+        out_specs=(VMEM,) * len(kinds),
         name="text_add",
         compiler_params=SMALL,
     )(own, other)
 
 
-def near_add_kernel(near, twice, out):
+def near_add_kernel(near, twice, *refs):
+    out = refs[-1]
     rows = near.shape[0]
     out[...] = (near[...] + twice[pl.ds(rows, rows)].astype(F32)).astype(BF16)
 
 
-def near_add(near, twice):
+def near_add(near, twice, after):
     return pl.pallas_call(
         near_add_kernel,
         out_shape=jax.ShapeDtypeStruct(near.shape, BF16),
-        in_specs=[VMEM] * 2,
+        in_specs=[VMEM] * 2 + [ANY] * len(after),
         out_specs=VMEM,
         name="near_add",
         compiler_params=SMALL,
-    )(near, twice)
+    )(near, twice, *after)
 
 
 def other_add_kernel(near, twice, out):
@@ -351,8 +353,8 @@
 
 def stats_kernel(mine, a, b, c, out):
     tail = pl.ds(a.shape[0] - STAT_ROWS, STAT_ROWS)
-    v = total_four(get_stats(mine), [get_stats(p.at[tail]) for p in (a, b, c)])
-    out[...] = v[:, :128]
+    v = total_four(mine[...], [get_stats(p.at[tail])[:, :128] for p in (a, b, c)])
+    out[...] = v
 
 
 def stats_sum(mine, parts):
@@ -378,9 +380,13 @@
             at.append(jnp.where(c, f * NX + s, s * NX + f))
     img = img[jnp.stack(at)].reshape(1, -1)
     up = 1 - 2 * c
+    sides = ((c, up), (1 - c, -up))
     at = []
-    for core, sign in ((c, up), (1 - c, -up)):
-        order = [(0, core), (4, core)] + [(k, d) for k in (1, 2, 3) for d in (core, 1 - core)]
+    for core, sign in sides:
+        order = [(0, core), (4, core), (1, core), (1, 1 - core)]
+        at += [(z - sign * k) % NZ * NC + d for k, d in order]
+    for core, sign in sides:
+        order = [(2, core), (2, 1 - core), (3, core), (3, 1 - core)]
         at += [(z - sign * k) % NZ * NC + d for k, d in order]
     txt = txt[jnp.stack(at)].reshape(-1, 1)
     return img, txt
@@ -402,30 +408,37 @@
     next_pair = hop_z(pair, 1)
     far = hop_z(yn, 4)
     near = join(near)
-    twice = hop_z(join([pair, next_pair]), 2)
+    twice = hop_z(join([pair, next_pair], [near]), 2)
     image_blocks = [near] + [hop_second(near, k) for k in (1, 2, 3)]
-    own = [yn, far, next_pair, twice]
-    other = [sibling, hop_core(join(own[1:]))]
+    early = [yn, far, next_pair, sibling, hop_core(join([far, next_pair]))]
+    late = [twice, hop_core(twice)]
 
     half = NZ * owned
-    g_own, gy_own, stats_own = tile(coef, img_ids, txt_ids[:half], image_blocks, own, F32)
-    g_other, gy_other, stats_other = tile(coef, img_ids, txt_ids[half:], image_blocks, other, BF16)
-
-    gy, far, near, twice = text_add(gy_own, hop_core(gy_other))
-    twice, far = hop_z(twice, -2), hop_z(far, 4)
-    near = hop_z(near_add(near, twice), -1)
-    text_parts = [gy, twice, near, far, hop_core(other_add(near, twice))]
-
-    keep, g1, g2, g3, stats = image_side(
-        own + other, [g_own, g_other], [stats_own, stats_other]
+    zero = jnp.zeros((3, 8, 128), F32)
+    g_early, keep_e, send_e, part = tile(
+        coef, img_ids, txt_ids[:half], zero, image_blocks, early, False
     )
+    g_late, keep_l, send_l, stats = tile(
+        coef, img_ids, txt_ids[half:], part, image_blocks, late, True
+    )
+
+    kinds = ((owned, F32), (owned, BF16), (2 * owned, F32))
+    gy, far, near_y = text_add(keep_e, hop_core(send_e), kinds)
+    (twice,) = text_add(keep_l, hop_core(send_l), ((4 * owned, BF16),))
+    stats = stats + exchange(stats, 5, 5)
+    keep, g1, g2, g3 = image_side(early + late, [g_early, g_late], [twice, far])
     parts = [hop_second(g, -k) for k, g in ((1, g1), (2, g2), (3, g3))]
-    keep, g1, g2, g3, stats = image_add(keep, parts, stats)
+
+    far, twice = hop_z(far, 4), hop_z(twice, -2)
+    near_y = hop_z(near_add(near_y, twice, [far]), -1)
+    text_parts = [gy, twice, near_y, far, hop_core(other_add(near_y, twice))]
+
+    for bits in ((1, 1), (2, 2), (6, 3), (7, 4)):
+        stats = stats + exchange(stats, *bits)
+    keep, g1, g2, g3 = image_add(keep, parts, stats)
     parts = [hop_first(g, -k) for k, g in ((1, g1), (2, g2), (3, g3))]
-
     stats = stats_sum(stats, parts)
-    for bit in (5, 1, 2, 0):
-        stats = stats + exchange(stats, bit)
+    stats = stats + exchange(stats, 0, 0)
     stats = stats[:, 0] * jnp.stack([jnp.float32(1 / LOG2E), scale[0], jnp.float32(1)])
 
     text_grad = finish(scale, texts, text_parts)

time: 190 us -> 161 us (0.85)
  waiting for transfers between devices: 88.7 us -> 50.6 us
  starting transfers between devices: 51.4 us -> 61.7 us
    ppermute x22 -> x24, waiting for transfers between devices: 79.1 us -> 34.3 us  [hop(): return lax.ppermute(a, ('row', 'col'), pairs)]
    ppermute x22 -> x24, starting transfers between devices: 41.7 us -> 49.2 us  [hop(): return lax.ppermute(a, ('row', 'col'), pairs)]
    ppermute x4 -> x6, waiting for transfers between devices: 9.54 us -> 16.2 us  [exchange(): return lax.ppermute(a, ('row', 'col'), pairs)]
    ppermute x4 -> x6, starting transfers between devices: 9.73 us -> 12.5 us  [exchange(): return lax.ppermute(a, ('row', 'col'), pairs)]
  transfers between devices with their start and end apart: 26 -> 30, of which waited for: 18 -> 12; matrix products, arithmetic and copies ran while one was open for 3% -> 4% of each run, Pallas kernels for 13% -> 22%
where the time goes in v1:
time: 161 us
  starting transfers between devices  61.7 us (38%)
  waiting for transfers between devices  50.6 us (31%)
  Pallas kernels  37.3 us (23%)
  local copies, waits for them, and re-layouts  7.97 us (5%)
  between operations  2.48 us (2%)
    ppermute x24, starting transfers between devices, hop(): return lax.ppermute(a, ('row', 'col'), pairs)  49.2 us
    ppermute x24, waiting for transfers between devices, hop(): return lax.ppermute(a, ('row', 'col'), pairs)  34.3 us
    pallas_call x2, Pallas kernels, tile(): pl.pallas_call(functools.partial(tile_kernel, len(images), len(texts), la...  23.2 us
    ppermute x6, waiting for transfers between devices, exchange(): return lax.ppermute(a, ('row', 'col'), pairs)  16.2 us
    ppermute x6, starting transfers between devices, exchange(): return lax.ppermute(a, ('row', 'col'), pairs)  12.5 us
    pallas_call x1, Pallas kernels, image_side(): pl.pallas_call(functools.partial(image_side_kernel, len(texts), len(grads...  9.04 us
  transfers between devices with their start and end apart: 30, of which 12 were waited for; matrix products, arithmetic and copies ran while one was open for 4% of the time, Pallas kernels for 22%

profile of v1, /device:TPU:1, one launch (start us, length us, event | category | flops | bytes accessed | tf_op | source)
XLA Modules:
  0.0 161.2 jit_solution(15804363292085778003)
XLA Ops:
  0.6 0.9 copy-done.5
  1.6 0.9 copy-done.8
  2.5 0.2 normalize.1
  2.7 3.3 %collective-permute-start.1 = (bf16[80,1152]{1,0:T(8,128)(2,1)S(1)}, bf16[80,1152]{1,0:T(8,128)(2,1)S(1)}, u32[]{:S(2)}, u32[]{:S(2)}) collective-permute-start(bf16[80,1152]{1,0:T(8,128)(2,1)S(1)} %get-tuple-element.24.refs_0_.refs_8_), channel_id=1, source_target_pairs={{0,1},{1,0},{32,33},{33,32},{2,3},{3,2},{34,35},{35,34},{4,5},{5,4... | collective-permute-start | bytes 552968 | tf_op jit(solution)/shard_map/ppermute | solution.py:31
  6.0 1.1 collective-permute-done.1.refs_1_.refs_11_.refs_3_
  7.0 0.5 join.4.refs_0_
  7.5 3.9 %collective-permute-start.2 = (bf16[160,1152]{1,0:T(8,128)(2,1)S(1)}, bf16[160,1152]{1,0:T(8,128)(2,1)S(1)}, u32[]{:S(2)}, u32[]{:S(2)}) collective-permute-start(bf16[160,1152]{1,0:T(8,128)(2,1)S(1)} %join.4.refs_0_), channel_id=1, source_target_pairs={{0,32},{1,39},{32,2},{33,1},{2,34},{3,33},{34,4},{35,3},{4,36},{5,... | collective-permute-start | bytes 1105928 | tf_op jit(solution)/shard_map/ppermute | solution.py:31
  11.4 2.7 %collective-permute-start.6 = (bf16[80,1152]{1,0:T(8,128)(2,1)S(1)}, bf16[80,1152]{1,0:T(8,128)(2,1)S(1)}, u32[]{:S(2)}, u32[]{:S(2)}) collective-permute-start(bf16[80,1152]{1,0:T(8,128)(2,1)S(1)} %get-tuple-element.25.refs_0_), channel_id=1, source_target_pairs={{0,24},{1,193},{32,56},{33,225},{2,26},{3,195},{34,58},{35,227},{4... | collective-permute-start | bytes 552968 | tf_op jit(solution)/shard_map/ppermute | solution.py:31
  14.2 0.3 collective-permute-start.5
  14.5 0.7 collective-permute-start.4
  15.2 3.4 %collective-permute-done.6.refs_3_ = bf16[80,1152]{1,0:T(8,128)(2,1)S(1)} collective-permute-done((bf16[80,1152]{1,0:T(8,128)(2,1)S(1)}, bf16[80,1152]{1,0:T(8,128)(2,1)S(1)}, u32[]{:S(2)}, u32[]{:S(2)}) %collective-permute-start.6) | collective-permute-done | bytes 184352 | tf_op jit(solution)/shard_map/ppermute | solution.py:31
  18.6 1.5 collective-permute-done.5.refs_2_
  20.2 1.9 %collective-permute-done.4.refs_1_ = bf16[80,1152]{1,0:T(8,128)(2,1)S(1)} collective-permute-done((bf16[80,1152]{1,0:T(8,128)(2,1)S(1)}, bf16[80,1152]{1,0:T(8,128)(2,1)S(1)}, u32[]{:S(2)}, u32[]{:S(2)}) %collective-permute-start.4) | collective-permute-done | bytes 184352 | tf_op jit(solution)/shard_map/ppermute | solution.py:31
  22.0 1.0 join.6.refs_2_.refs_4_
  23.1 0.3 join.7
  23.4 1.5 collective-permute-start.7
  25.0 0.4 collective-permute-start
  25.3 0.3 reshape.1255
  25.6 0.3 reshape.1257
  26.0 0.1 stack.138
  26.1 0.1 stack.121
  26.3 2.3 %collective-permute-start.11 = (bf16[320,1152]{1,0:T(8,128)(2,1)S(1)}, bf16[320,1152]{1,0:T(8,128)(2,1)}, u32[]{:S(2)}, u32[]{:S(2)}) collective-permute-start(bf16[320,1152]{1,0:T(8,128)(2,1)S(1)} %join.6.refs_2_.refs_4_), channel_id=1, source_target_pairs={{0,192},{1,25},{32,224},{33,57},{2,194},{3,27},{34,226},{35,59},{4... | collective-permute-start | bytes 2211848 | tf_op jit(solution)/shard_map/ppermute | solution.py:31
  28.5 0.5 collective-permute-start.10
  29.1 0.6 collective-permute-start.9
  29.7 10.7 %collective-permute-done.refs_0_.refs_9_.refs_1_ = bf16[80,1152]{1,0:T(8,128)(2,1)S(1)} collective-permute-done((bf16[80,1152]{1,0:T(8,128)(2,1)S(1)}, bf16[80,1152]{1,0:T(8,128)(2,1)S(1)}, u32[]{:S(2)}, u32[]{:S(2)}) %collective-permute-start) | collective-permute-done | bytes 184352 | tf_op jit(solution)/shard_map/ppermute | solution.py:31
  40.4 0.4 join.5
  40.8 10.8 %collective-permute-start.3 = (bf16[240,1152]{1,0:T(8,128)(2,1)S(1)}, bf16[240,1152]{1,0:T(8,128)(2,1)}, u32[]{:S(2)}, u32[]{:S(2)}) collective-permute-start(bf16[240,1152]{1,0:T(8,128)(2,1)S(1)} %join.5), channel_id=1, source_target_pairs={{0,1},{1,0},{32,33},{33,32},{2,3},{3,2},{34,35},{35,34},{4,5},{5,4... | collective-permute-start | bytes 1658888 | tf_op jit(solution)/shard_map/ppermute | solution.py:31
  51.7 0.3 collective-permute-start.8
  53.3 0.6 gather_fusion
  53.9 0.7 reshape.1256.refs_1_
  54.6 0.6 gather_fusion.1
  55.1 0.9 slice.21.refs_2_
  56.0 0.9 slice.20.refs_2_
  56.9 0.6 pad_maximum_fusion.refs_0_
  57.5 0.6 broadcast_in_dim.2.refs_3_
  58.1 11.5 %tile_early.1 = (bf16[640,1280]{1,0:T(8,128)(2,1)}, f32[320,1152]{1,0:T(8,128)}, bf16[320,1152]{1,0:T(8,128)(2,1)}, f32[3,8,128]{2,1,0:T(8,128)}) custom-call(f32[2]{0:T(128)} %pad_maximum_fusion.refs_0_, s32[1,1280]{1,0:T(1,128)} %reshape.1256.refs_1_, s32[640,1]{1,0:T(8,128)} %slice.20.refs_2_, f32[3,8,128]{2,1,0:T(8,128)} %broadcast_in_dim.2.refs_3_, ...), custom_call_target="tpu_custom_call" | custom-call | flops 3774873600 | bytes 11796480 | tf_op jit(solution)/shard_map/tile_early/pallas_call | solution.py:192
  69.6 0.6 collective-permute-start.13
  70.2 0.9 copy-done.19
  71.2 11.6 %tile_late.1 = (bf16[640,1280]{1,0:T(8,128)(2,1)}, f32[320,1152]{1,0:T(8,128)}, bf16[320,1152]{1,0:T(8,128)(2,1)}, f32[3,128]{1,0:T(4,128)}) custom-call(f32[2]{0:T(128)} %pad_maximum_fusion.refs_0_, s32[1,1280]{1,0:T(1,128)} %reshape.1256.refs_1_, s32[640,1]{1,0:T(8,128)} %slice.21.refs_2_, f32[3,8,128]{2,1,0:T(8,128)} %get-tuple-element.27.refs_3_, ...), custom_call_target="tpu_custom_call" | custom-call | flops 3774873600 | bytes 11796480 | tf_op jit(solution)/shard_map/tile_late/pallas_call | solution.py:192
  82.8 0.1 collective-permute-start.12
  82.9 0.1 text_add.3
  83.1 2.3 %collective-permute-done.12.other = bf16[320,1152]{1,0:T(8,128)(2,1)S(1)} collective-permute-done((bf16[320,1152]{1,0:T(8,128)(2,1)}, bf16[320,1152]{1,0:T(8,128)(2,1)S(1)}, u32[]{:S(2)}, u32[]{:S(2)}) %collective-permute-start.12) | collective-permute-done | bytes 737312 | tf_op jit(solution)/shard_map/ppermute | solution.py:31
  85.3 0.2 text_add.2.refs_9_
  85.5 3.1 %collective-permute-start.25 = (bf16[320,1152]{1,0:T(8,128)(2,1)S(1)}, bf16[320,1152]{1,0:T(8,128)(2,1)S(1)}, u32[]{:S(2)}, u32[]{:S(2)}) collective-permute-start(bf16[320,1152]{1,0:T(8,128)(2,1)S(1)} %text_add.2.refs_9_), channel_id=1, source_target_pairs={{0,6},{1,3},{32,38},{33,35},{2,0},{3,5},{34,32},{35,37},{4,2},{5,7... | collective-permute-start | bytes 2211848 | tf_op jit(solution)/shard_map/ppermute | solution.py:31
  88.7 9.0 %image_side.1 = (f32[320,1152]{1,0:T(8,128)}, bf16[320,1152]{1,0:T(8,128)(2,1)}, bf16[320,1152]{1,0:T(8,128)(2,1)}, bf16[320,1152]{1,0:T(8,128)(2,1)}) custom-call(bf16[80,1152]{1,0:T(8,128)(2,1)} %copy-done.10, bf16[80,1152]{1,0:T(8,128)(2,1)} %copy-done.12, bf16[160,1152]{1,0:T(8,128)(2,1)} %copy-done.4, bf16[80,1152]{1,0:T(8,128)(2,1)} %copy-done.11, ...), custom_call_target="tpu_custom_call" | custom-call | flops 3774873600 | bytes 11796480 | tf_op jit(solution)/shard_map/image_side/pallas_call | solution.py:233
  97.9 1.4 collective-permute-start.16
  99.3 4.8 %collective-permute-start.26 = (bf16[80,1152]{1,0:T(8,128)(2,1)S(1)}, bf16[80,1152]{1,0:T(8,128)(2,1)S(1)}, u32[]{:S(2)}, u32[]{:S(2)}) collective-permute-start(bf16[80,1152]{1,0:T(8,128)(2,1)S(1)} %copy-done.14), channel_id=1, source_target_pairs={{0,4},{1,5},{32,36},{33,37},{2,6},{3,7},{34,38},{35,39},{4,0},{5,1... | collective-permute-start | bytes 552968 | tf_op jit(solution)/shard_map/ppermute | solution.py:31
  104.1 13.4 %collective-permute-done.26.refs_0_.refs_4_ = bf16[80,1152]{1,0:T(8,128)(2,1)S(1)} collective-permute-done((bf16[80,1152]{1,0:T(8,128)(2,1)S(1)}, bf16[80,1152]{1,0:T(8,128)(2,1)S(1)}, u32[]{:S(2)}, u32[]{:S(2)}) %collective-permute-start.26) | collective-permute-done | bytes 184352 | tf_op jit(solution)/shard_map/ppermute | solution.py:31
  117.8 4.4 %collective-permute-done.17 = f32[3,128]{1,0:T(4,128)S(1)} collective-permute-done((f32[3,128]{1,0:T(4,128)S(1)}, f32[3,128]{1,0:T(4,128)S(1)}, u32[]{:S(2)}, u32[]{:S(2)}) %collective-permute-start.17) | collective-permute-done | bytes 1568 | tf_op jit(solution)/shard_map/ppermute | solution.py:52
  122.2 0.8 collective-permute-start.18
  123.0 2.5 %collective-permute-done.18 = f32[3,128]{1,0:T(4,128)S(1)} collective-permute-done((f32[3,128]{1,0:T(4,128)S(1)}, f32[3,128]{1,0:T(4,128)S(1)}, u32[]{:S(2)}, u32[]{:S(2)}) %collective-permute-start.18) | collective-permute-done | bytes 1568 | tf_op jit(solution)/shard_map/ppermute | solution.py:52
  125.6 1.9 %collective-permute-start.19 = (f32[3,128]{1,0:T(4,128)S(1)}, f32[3,128]{1,0:T(4,128)S(1)}, u32[]{:S(2)}, u32[]{:S(2)}) collective-permute-start(f32[3,128]{1,0:T(4,128)S(1)} %add.383), channel_id=1, source_target_pairs={{0,4},{1,5},{2,6},{3,7},{4,0},{5,1},{6,2},{7,3},{8,12},{9,13},{10,... | collective-permute-start | bytes 4616 | tf_op jit(solution)/shard_map/ppermute | solution.py:52
  127.5 4.4 %collective-permute-done.19 = f32[3,128]{1,0:T(4,128)S(1)} collective-permute-done((f32[3,128]{1,0:T(4,128)S(1)}, f32[3,128]{1,0:T(4,128)S(1)}, u32[]{:S(2)}, u32[]{:S(2)}) %collective-permute-start.19) | collective-permute-done | bytes 1568 | tf_op jit(solution)/shard_map/ppermute | solution.py:52
  132.0 2.4 %collective-permute-done.20 = f32[3,128]{1,0:T(4,128)S(1)} collective-permute-done((f32[3,128]{1,0:T(4,128)S(1)}, f32[3,128]{1,0:T(4,128)S(1)}, u32[]{:S(2)}, u32[]{:S(2)}) %collective-permute-start.20) | collective-permute-done | bytes 1568 | tf_op jit(solution)/shard_map/ppermute | solution.py:52
  134.4 1.4 collective-permute-start.21
  135.8 2.5 %collective-permute-done.21 = f32[3,128]{1,0:T(4,128)S(1)} collective-permute-done((f32[3,128]{1,0:T(4,128)S(1)}, f32[3,128]{1,0:T(4,128)S(1)}, u32[]{:S(2)}, u32[]{:S(2)}) %collective-permute-start.21) | collective-permute-done | bytes 1568 | tf_op jit(solution)/shard_map/ppermute | solution.py:52
  138.3 0.5 image_add.1
  139.1 1.3 collective-permute-start.24
  140.5 9.9 %collective-permute-start.28 = (f32[80,1152]{1,0:T(8,128)S(1)}, f32[80,1152]{1,0:T(8,128)S(1)}, u32[]{:S(2)}, u32[]{:S(2)}) collective-permute-start(f32[80,1152]{1,0:T(8,128)S(1)} %other_add.1), channel_id=1, source_target_pairs={{0,1},{1,0},{32,33},{33,32},{2,3},{3,2},{34,35},{35,34},{4,5},{5,4... | collective-permute-start | bytes 1105928 | tf_op jit(solution)/shard_map/ppermute | solution.py:31
  150.4 8.2 %collective-permute-start.29 = (f32[3,128]{1,0:T(4,128)S(1)}, f32[3,128]{1,0:T(4,128)S(1)}, u32[]{:S(2)}, u32[]{:S(2)}) collective-permute-start(f32[3,128]{1,0:T(4,128)S(1)} %stats_sum.1), channel_id=1, source_target_pairs={{0,1},{1,0},{2,3},{3,2},{4,5},{5,4},{6,7},{7,6},{8,9},{9,8},{10,11... | collective-permute-start | bytes 4616 | tf_op jit(solution)/shard_map/ppermute | solution.py:52
  158.6 0.9 finish.2
  159.6 0.1 slice_reduce_fusion
  159.7 0.6 fusion.2
  160.3 0.9 finish.3
  (78 shorter events, 0.9 us)
Async XLA Ops:
  0.6 0.9 copy-start.5
  1.6 0.9 copy-start.8
  2.6 22.3 %copy-start.10 = (bf16[80,1152]{1,0:T(8,128)(2,1)}, bf16[80,1152]{1,0:T(8,128)(2,1)S(1)}, u32[]{:S(2)}) copy-start(bf16[80,1152]{1,0:T(8,128)(2,1)S(1)} %get-tuple-element.24.refs_0_.refs_8_) | copy-start | bytes 552964
  2.7 4.4 %collective-permute-start.1 = (bf16[80,1152]{1,0:T(8,128)(2,1)S(1)}, bf16[80,1152]{1,0:T(8,128)(2,1)S(1)}, u32[]{:S(2)}, u32[]{:S(2)}) collective-permute-start(bf16[80,1152]{1,0:T(8,128)(2,1)S(1)} %get-tuple-element.24.refs_0_.refs_8_), channel_id=1, source_target_pairs={{0,1},{1,0},{32,33},{33,32},{2,3},{3,2},{34,35},{35,34},{4,5},{5,4... | collective-permute-start | bytes 552968 | tf_op jit(solution)/shard_map/ppermute | solution.py:31
  7.0 16.4 %copy-start.11 = (bf16[80,1152]{1,0:T(8,128)(2,1)}, bf16[80,1152]{1,0:T(8,128)(2,1)S(1)}, u32[]{:S(2)}) copy-start(bf16[80,1152]{1,0:T(8,128)(2,1)S(1)} %collective-permute-done.1.refs_1_.refs_11_.refs_3_) | copy-start | bytes 552964
  7.5 15.5 %collective-permute-start.2 = (bf16[160,1152]{1,0:T(8,128)(2,1)S(1)}, bf16[160,1152]{1,0:T(8,128)(2,1)S(1)}, u32[]{:S(2)}, u32[]{:S(2)}) collective-permute-start(bf16[160,1152]{1,0:T(8,128)(2,1)S(1)} %join.4.refs_0_), channel_id=1, source_target_pairs={{0,32},{1,39},{32,2},{33,1},{2,34},{3,33},{34,4},{35,3},{4,36},{5,... | collective-permute-start | bytes 1105928 | tf_op jit(solution)/shard_map/ppermute | solution.py:31
  11.4 7.2 %collective-permute-start.6 = (bf16[80,1152]{1,0:T(8,128)(2,1)S(1)}, bf16[80,1152]{1,0:T(8,128)(2,1)S(1)}, u32[]{:S(2)}, u32[]{:S(2)}) collective-permute-start(bf16[80,1152]{1,0:T(8,128)(2,1)S(1)} %get-tuple-element.25.refs_0_), channel_id=1, source_target_pairs={{0,24},{1,193},{32,56},{33,225},{2,26},{3,195},{34,58},{35,227},{4... | collective-permute-start | bytes 552968 | tf_op jit(solution)/shard_map/ppermute | solution.py:31
  14.2 6.0 %collective-permute-start.5 = (bf16[80,1152]{1,0:T(8,128)(2,1)S(1)}, bf16[80,1152]{1,0:T(8,128)(2,1)S(1)}, u32[]{:S(2)}, u32[]{:S(2)}) collective-permute-start(bf16[80,1152]{1,0:T(8,128)(2,1)S(1)} %get-tuple-element.25.refs_0_), channel_id=1, source_target_pairs={{0,16},{1,129},{32,48},{33,161},{2,18},{3,131},{34,50},{35,163},{4... | collective-permute-start | bytes 552968 | tf_op jit(solution)/shard_map/ppermute | solution.py:31
  14.5 7.5 %collective-permute-start.4 = (bf16[80,1152]{1,0:T(8,128)(2,1)S(1)}, bf16[80,1152]{1,0:T(8,128)(2,1)S(1)}, u32[]{:S(2)}, u32[]{:S(2)}) collective-permute-start(bf16[80,1152]{1,0:T(8,128)(2,1)S(1)} %get-tuple-element.25.refs_0_), channel_id=1, source_target_pairs={{0,8},{1,65},{32,40},{33,97},{2,10},{3,67},{34,42},{35,99},{4,12},... | collective-permute-start | bytes 552968 | tf_op jit(solution)/shard_map/ppermute | solution.py:31
  23.0 6.1 %copy-start = (bf16[320,1152]{1,0:T(8,128)(2,1)}, bf16[320,1152]{1,0:T(8,128)(2,1)S(1)}, u32[]{:S(2)}) copy-start(bf16[320,1152]{1,0:T(8,128)(2,1)S(1)} %join.6.refs_2_.refs_4_) | copy-start | bytes 2211844
  23.0 2.3 %copy-start.15 = (s32[20480]{0:T(1024)S(1)}, s32[20480]{0:T(1024)}, u32[]{:S(2)}) copy-start(s32[20480]{0:T(1024)} %param.8) | copy-start | bytes 245764
  23.0 2.6 %copy-start.16 = (s32[20480]{0:T(1024)S(1)}, s32[20480]{0:T(1024)}, u32[]{:S(2)}) copy-start(s32[20480]{0:T(1024)} %param.9) | copy-start | bytes 245764
  23.1 17.3 %copy-start.4 = (bf16[160,1152]{1,0:T(8,128)(2,1)}, bf16[160,1152]{1,0:T(8,128)(2,1)S(1)}, u32[]{:S(2)}) copy-start(bf16[160,1152]{1,0:T(8,128)(2,1)S(1)} %collective-permute-done.2.refs_1_.refs_10_.refs_2_) | copy-start | bytes 1105924
  23.4 28.2 %collective-permute-start.7 = (bf16[320,1152]{1,0:T(8,128)(2,1)S(1)}, bf16[320,1152]{1,0:T(8,128)(2,1)S(1)}, u32[]{:S(2)}, u32[]{:S(2)}) collective-permute-start(bf16[320,1152]{1,0:T(8,128)(2,1)S(1)} %join.7), channel_id=1, source_target_pairs={{0,2},{1,7},{32,34},{33,39},{2,4},{3,1},{34,36},{35,33},{4,6},{5,3... | collective-permute-start | bytes 2211848 | tf_op jit(solution)/shard_map/ppermute | solution.py:31
  25.0 15.4 %collective-permute-start = (bf16[80,1152]{1,0:T(8,128)(2,1)S(1)}, bf16[80,1152]{1,0:T(8,128)(2,1)S(1)}, u32[]{:S(2)}, u32[]{:S(2)}) collective-permute-start(bf16[80,1152]{1,0:T(8,128)(2,1)S(1)} %get-tuple-element.24.refs_0_.refs_8_), channel_id=1, source_target_pairs={{0,4},{1,5},{32,36},{33,37},{2,6},{3,7},{34,38},{35,39},{4,0},{5,1... | collective-permute-start | bytes 552968 | tf_op jit(solution)/shard_map/ppermute | solution.py:31
  26.3 31.2 %collective-permute-start.11 = (bf16[320,1152]{1,0:T(8,128)(2,1)S(1)}, bf16[320,1152]{1,0:T(8,128)(2,1)}, u32[]{:S(2)}, u32[]{:S(2)}) collective-permute-start(bf16[320,1152]{1,0:T(8,128)(2,1)S(1)} %join.6.refs_2_.refs_4_), channel_id=1, source_target_pairs={{0,192},{1,25},{32,224},{33,57},{2,194},{3,27},{34,226},{35,59},{4... | collective-permute-start | bytes 2211848 | tf_op jit(solution)/shard_map/ppermute | solution.py:31
  28.5 29.0 %collective-permute-start.10 = (bf16[320,1152]{1,0:T(8,128)(2,1)S(1)}, bf16[320,1152]{1,0:T(8,128)(2,1)}, u32[]{:S(2)}, u32[]{:S(2)}) collective-permute-start(bf16[320,1152]{1,0:T(8,128)(2,1)S(1)} %join.6.refs_2_.refs_4_), channel_id=1, source_target_pairs={{0,128},{1,17},{32,160},{33,49},{2,130},{3,19},{34,162},{35,51},{4... | collective-permute-start | bytes 2211848 | tf_op jit(solution)/shard_map/ppermute | solution.py:31
  29.1 28.4 %collective-permute-start.9 = (bf16[320,1152]{1,0:T(8,128)(2,1)S(1)}, bf16[320,1152]{1,0:T(8,128)(2,1)}, u32[]{:S(2)}, u32[]{:S(2)}) collective-permute-start(bf16[320,1152]{1,0:T(8,128)(2,1)S(1)} %join.6.refs_2_.refs_4_), channel_id=1, source_target_pairs={{0,64},{1,9},{32,96},{33,41},{2,66},{3,11},{34,98},{35,43},{4,68},... | collective-permute-start | bytes 2211848 | tf_op jit(solution)/shard_map/ppermute | solution.py:31
  40.4 17.7 %copy-start.12 = (bf16[80,1152]{1,0:T(8,128)(2,1)}, bf16[80,1152]{1,0:T(8,128)(2,1)S(1)}, u32[]{:S(2)}) copy-start(bf16[80,1152]{1,0:T(8,128)(2,1)S(1)} %collective-permute-done.refs_0_.refs_9_.refs_1_) | copy-start | bytes 552964
  40.8 16.7 %collective-permute-start.3 = (bf16[240,1152]{1,0:T(8,128)(2,1)S(1)}, bf16[240,1152]{1,0:T(8,128)(2,1)}, u32[]{:S(2)}, u32[]{:S(2)}) collective-permute-start(bf16[240,1152]{1,0:T(8,128)(2,1)S(1)} %join.5), channel_id=1, source_target_pairs={{0,1},{1,0},{32,33},{33,32},{2,3},{3,2},{34,35},{35,34},{4,5},{5,4... | collective-permute-start | bytes 1658888 | tf_op jit(solution)/shard_map/ppermute | solution.py:31
  51.7 18.0 %copy-start.18 = (bf16[320,1152]{1,0:T(8,128)(2,1)}, bf16[320,1152]{1,0:T(8,128)(2,1)S(1)}, u32[]{:S(2)}) copy-start(bf16[320,1152]{1,0:T(8,128)(2,1)S(1)} %collective-permute-done.7.refs_8_.refs_5_) | copy-start | bytes 2211844
  51.7 18.6 %collective-permute-start.8 = (bf16[320,1152]{1,0:T(8,128)(2,1)S(1)}, bf16[320,1152]{1,0:T(8,128)(2,1)S(1)}, u32[]{:S(2)}, u32[]{:S(2)}) collective-permute-start(bf16[320,1152]{1,0:T(8,128)(2,1)S(1)} %collective-permute-done.7.refs_8_.refs_5_), channel_id=1, source_target_pairs={{0,1},{1,0},{32,33},{33,32},{2,3},{3,2},{34,35},{35,34},{4,5},{5,4... | collective-permute-start | bytes 2211848 | tf_op jit(solution)/shard_map/ppermute | solution.py:31
  69.6 13.3 %collective-permute-start.13 = (bf16[320,1152]{1,0:T(8,128)(2,1)}, bf16[320,1152]{1,0:T(8,128)(2,1)S(1)}, u32[]{:S(2)}, u32[]{:S(2)}) collective-permute-start(bf16[320,1152]{1,0:T(8,128)(2,1)} %get-tuple-element.32), channel_id=1, source_target_pairs={{0,1},{1,0},{32,33},{33,32},{2,3},{3,2},{34,35},{35,34},{4,5},{5,4... | collective-permute-start | bytes 2211848 | tf_op jit(solution)/shard_map/ppermute | solution.py:31
  70.2 0.9 copy-start.19
  71.2 11.8 %copy-start.2 = (f32[320,1152]{1,0:T(8,128)S(1)}, f32[320,1152]{1,0:T(8,128)}, u32[]{:S(2)}) copy-start(f32[320,1152]{1,0:T(8,128)} %get-tuple-element.31.own) | copy-start | bytes 4423684
  82.8 2.5 %copy-start.3 = (f32[320,1152]{1,0:T(8,128)S(1)}, f32[320,1152]{1,0:T(8,128)}, u32[]{:S(2)}) copy-start(f32[320,1152]{1,0:T(8,128)} %get-tuple-element.29.own) | copy-start | bytes 4423684
  82.8 2.5 %collective-permute-start.12 = (bf16[320,1152]{1,0:T(8,128)(2,1)}, bf16[320,1152]{1,0:T(8,128)(2,1)S(1)}, u32[]{:S(2)}, u32[]{:S(2)}) collective-permute-start(bf16[320,1152]{1,0:T(8,128)(2,1)} %get-tuple-element.30), channel_id=1, source_target_pairs={{0,1},{1,0},{32,33},{33,32},{2,3},{3,2},{34,35},{35,34},{4,5},{5,4... | collective-permute-start | bytes 2211848 | tf_op jit(solution)/shard_map/ppermute | solution.py:31
  83.1 2.4 %copy-start.13 = (bf16[80,1152]{1,0:T(8,128)(2,1)}, bf16[80,1152]{1,0:T(8,128)(2,1)S(1)}, u32[]{:S(2)}) copy-start(bf16[80,1152]{1,0:T(8,128)(2,1)S(1)} %get-tuple-element.33.refs_10_) | copy-start | bytes 552964
  85.5 3.2 %copy-start.7 = (bf16[320,1152]{1,0:T(8,128)(2,1)}, bf16[320,1152]{1,0:T(8,128)(2,1)S(1)}, u32[]{:S(2)}) copy-start(bf16[320,1152]{1,0:T(8,128)(2,1)S(1)} %text_add.2.refs_9_) | copy-start | bytes 2211844
  85.5 32.0 %collective-permute-start.25 = (bf16[320,1152]{1,0:T(8,128)(2,1)S(1)}, bf16[320,1152]{1,0:T(8,128)(2,1)S(1)}, u32[]{:S(2)}, u32[]{:S(2)}) collective-permute-start(bf16[320,1152]{1,0:T(8,128)(2,1)S(1)} %text_add.2.refs_9_), channel_id=1, source_target_pairs={{0,6},{1,3},{32,38},{33,35},{2,0},{3,5},{34,32},{35,37},{4,2},{5,7... | collective-permute-start | bytes 2211848 | tf_op jit(solution)/shard_map/ppermute | solution.py:31
  88.7 10.6 %copy-start.14 = (bf16[80,1152]{1,0:T(8,128)(2,1)S(1)}, bf16[80,1152]{1,0:T(8,128)(2,1)}, u32[]{:S(2)}) copy-start(bf16[80,1152]{1,0:T(8,128)(2,1)} %copy-done.13) | copy-start | bytes 552964
  97.7 20.0 %copy-start.17 = (f32[3,128]{1,0:T(4,128)S(1)}, f32[3,128]{1,0:T(4,128)}, u32[]{:S(2)}) copy-start(f32[3,128]{1,0:T(4,128)} %get-tuple-element.38) | copy-start | bytes 4612
  97.7 40.6 %copy-start.1 = (f32[320,1152]{1,0:T(8,128)S(1)}, f32[320,1152]{1,0:T(8,128)}, u32[]{:S(2)}) copy-start(f32[320,1152]{1,0:T(8,128)} %get-tuple-element.34.own) | copy-start | bytes 4423684
  97.7 40.6 %collective-permute-start.14 = (bf16[320,1152]{1,0:T(8,128)(2,1)}, bf16[320,1152]{1,0:T(8,128)(2,1)S(1)}, u32[]{:S(2)}, u32[]{:S(2)}) collective-permute-start(bf16[320,1152]{1,0:T(8,128)(2,1)} %get-tuple-element.35), channel_id=1, source_target_pairs={{0,192},{1,25},{32,224},{33,57},{2,194},{3,27},{34,226},{35,59},{4... | collective-permute-start | bytes 2211848 | tf_op jit(solution)/shard_map/ppermute | solution.py:31
  97.8 40.5 %collective-permute-start.15 = (bf16[320,1152]{1,0:T(8,128)(2,1)}, bf16[320,1152]{1,0:T(8,128)(2,1)S(1)}, u32[]{:S(2)}, u32[]{:S(2)}) collective-permute-start(bf16[320,1152]{1,0:T(8,128)(2,1)} %get-tuple-element.36), channel_id=1, source_target_pairs={{0,128},{1,17},{32,160},{33,49},{2,130},{3,19},{34,162},{35,51},{4... | collective-permute-start | bytes 2211848 | tf_op jit(solution)/shard_map/ppermute | solution.py:31
  97.9 40.4 %collective-permute-start.16 = (bf16[320,1152]{1,0:T(8,128)(2,1)}, bf16[320,1152]{1,0:T(8,128)(2,1)S(1)}, u32[]{:S(2)}, u32[]{:S(2)}) collective-permute-start(bf16[320,1152]{1,0:T(8,128)(2,1)} %get-tuple-element.37), channel_id=1, source_target_pairs={{0,64},{1,9},{32,96},{33,41},{2,66},{3,11},{34,98},{35,43},{4,68},... | collective-permute-start | bytes 2211848 | tf_op jit(solution)/shard_map/ppermute | solution.py:31
  99.3 18.3 %collective-permute-start.26 = (bf16[80,1152]{1,0:T(8,128)(2,1)S(1)}, bf16[80,1152]{1,0:T(8,128)(2,1)S(1)}, u32[]{:S(2)}, u32[]{:S(2)}) collective-permute-start(bf16[80,1152]{1,0:T(8,128)(2,1)S(1)} %copy-done.14), channel_id=1, source_target_pairs={{0,4},{1,5},{32,36},{33,37},{2,6},{3,7},{34,38},{35,39},{4,0},{5,1... | collective-permute-start | bytes 552968 | tf_op jit(solution)/shard_map/ppermute | solution.py:31
  117.6 22.8 %collective-permute-start.27 = (bf16[160,1152]{1,0:T(8,128)(2,1)S(1)}, bf16[160,1152]{1,0:T(8,128)(2,1)S(1)}, u32[]{:S(2)}, u32[]{:S(2)}) collective-permute-start(bf16[160,1152]{1,0:T(8,128)(2,1)S(1)} %near_add.1), channel_id=1, source_target_pairs={{0,38},{1,33},{32,0},{33,3},{2,32},{3,35},{34,2},{35,5},{4,34},{5,... | collective-permute-start | bytes 1105928 | tf_op jit(solution)/shard_map/ppermute | solution.py:31
  117.7 4.5 %collective-permute-start.17 = (f32[3,128]{1,0:T(4,128)S(1)}, f32[3,128]{1,0:T(4,128)S(1)}, u32[]{:S(2)}, u32[]{:S(2)}) collective-permute-start(f32[3,128]{1,0:T(4,128)S(1)} %copy-done.17), channel_id=1, source_target_pairs={{0,32},{1,33},{2,34},{3,35},{4,36},{5,37},{6,38},{7,39},{8,40},{9,... | collective-permute-start | bytes 4616 | tf_op jit(solution)/shard_map/ppermute | solution.py:52
  122.2 3.3 %collective-permute-start.18 = (f32[3,128]{1,0:T(4,128)S(1)}, f32[3,128]{1,0:T(4,128)S(1)}, u32[]{:S(2)}, u32[]{:S(2)}) collective-permute-start(f32[3,128]{1,0:T(4,128)S(1)} %add.382), channel_id=1, source_target_pairs={{0,2},{1,3},{2,0},{3,1},{4,6},{5,7},{6,4},{7,5},{8,10},{9,11},{10,... | collective-permute-start | bytes 4616 | tf_op jit(solution)/shard_map/ppermute | solution.py:52
  125.6 6.3 %collective-permute-start.19 = (f32[3,128]{1,0:T(4,128)S(1)}, f32[3,128]{1,0:T(4,128)S(1)}, u32[]{:S(2)}, u32[]{:S(2)}) collective-permute-start(f32[3,128]{1,0:T(4,128)S(1)} %add.383), channel_id=1, source_target_pairs={{0,4},{1,5},{2,6},{3,7},{4,0},{5,1},{6,2},{7,3},{8,12},{9,13},{10,... | collective-permute-start | bytes 4616 | tf_op jit(solution)/shard_map/ppermute | solution.py:52
  131.9 2.4 %collective-permute-start.20 = (f32[3,128]{1,0:T(4,128)S(1)}, f32[3,128]{1,0:T(4,128)S(1)}, u32[]{:S(2)}, u32[]{:S(2)}) collective-permute-start(f32[3,128]{1,0:T(4,128)S(1)} %add.384), channel_id=1, source_target_pairs={{0,64},{1,9},{2,66},{3,11},{4,68},{5,13},{6,70},{7,15},{8,72},{9,1... | collective-permute-start | bytes 4616 | tf_op jit(solution)/shard_map/ppermute | solution.py:52
  134.4 3.9 %collective-permute-start.21 = (f32[3,128]{1,0:T(4,128)S(1)}, f32[3,128]{1,0:T(4,128)S(1)}, u32[]{:S(2)}, u32[]{:S(2)}) collective-permute-start(f32[3,128]{1,0:T(4,128)S(1)} %add.385), channel_id=1, source_target_pairs={{0,128},{1,17},{2,130},{3,19},{4,132},{5,21},{6,134},{7,23},{8,136... | collective-permute-start | bytes 4616 | tf_op jit(solution)/shard_map/ppermute | solution.py:52
  138.9 19.8 %copy-start.6 = (bf16[80,1152]{1,0:T(8,128)(2,1)S(1)}, bf16[80,1152]{1,0:T(8,128)(2,1)}, u32[]{:S(2)}) copy-start(bf16[80,1152]{1,0:T(8,128)(2,1)} %refs_0_.2) | copy-start | bytes 552964
  138.9 11.5 %collective-permute-start.22 = (bf16[96,1152]{1,0:T(8,128)(2,1)S(1)}, bf16[96,1152]{1,0:T(8,128)(2,1)S(1)}, u32[]{:S(2)}, u32[]{:S(2)}) collective-permute-start(bf16[96,1152]{1,0:T(8,128)(2,1)S(1)} %get-tuple-element.40), channel_id=1, source_target_pairs={{0,24},{1,193},{32,56},{33,225},{2,26},{3,195},{34,58},{35,227},{4... | collective-permute-start | bytes 663560 | tf_op jit(solution)/shard_map/ppermute | solution.py:31
  139.0 11.4 %collective-permute-start.23 = (bf16[96,1152]{1,0:T(8,128)(2,1)S(1)}, bf16[96,1152]{1,0:T(8,128)(2,1)S(1)}, u32[]{:S(2)}, u32[]{:S(2)}) collective-permute-start(bf16[96,1152]{1,0:T(8,128)(2,1)S(1)} %get-tuple-element.41), channel_id=1, source_target_pairs={{0,16},{1,129},{32,48},{33,161},{2,18},{3,131},{34,50},{35,163},{4... | collective-permute-start | bytes 663560 | tf_op jit(solution)/shard_map/ppermute | solution.py:31
  139.1 21.2 %copy-start.9 = (bf16[80,1152]{1,0:T(8,128)(2,1)S(1)}, bf16[80,1152]{1,0:T(8,128)(2,1)}, u32[]{:S(2)}) copy-start(bf16[80,1152]{1,0:T(8,128)(2,1)} %refs_0_.3) | copy-start | bytes 552964
  139.1 11.3 %collective-permute-start.24 = (bf16[96,1152]{1,0:T(8,128)(2,1)S(1)}, bf16[96,1152]{1,0:T(8,128)(2,1)S(1)}, u32[]{:S(2)}, u32[]{:S(2)}) collective-permute-start(bf16[96,1152]{1,0:T(8,128)(2,1)S(1)} %get-tuple-element.42), channel_id=1, source_target_pairs={{0,8},{1,65},{32,40},{33,97},{2,10},{3,67},{34,42},{35,99},{4,12},... | collective-permute-start | bytes 663560 | tf_op jit(solution)/shard_map/ppermute | solution.py:31
  140.5 19.8 %collective-permute-start.28 = (f32[80,1152]{1,0:T(8,128)S(1)}, f32[80,1152]{1,0:T(8,128)S(1)}, u32[]{:S(2)}, u32[]{:S(2)}) collective-permute-start(f32[80,1152]{1,0:T(8,128)S(1)} %other_add.1), channel_id=1, source_target_pairs={{0,1},{1,0},{32,33},{33,32},{2,3},{3,2},{34,35},{35,34},{4,5},{5,4... | collective-permute-start | bytes 1105928 | tf_op jit(solution)/shard_map/ppermute | solution.py:31
  150.4 9.1 %collective-permute-start.29 = (f32[3,128]{1,0:T(4,128)S(1)}, f32[3,128]{1,0:T(4,128)S(1)}, u32[]{:S(2)}, u32[]{:S(2)}) collective-permute-start(f32[3,128]{1,0:T(4,128)S(1)} %stats_sum.1), channel_id=1, source_target_pairs={{0,1},{1,0},{2,3},{3,2},{4,5},{5,4},{6,7},{7,6},{8,9},{9,8},{10,11... | collective-permute-start | bytes 4616 | tf_op jit(solution)/shard_map/ppermute | solution.py:52
